TPU v7x, 32 devices: a whole 2x2x4 slice. The times are simulated.
32 devices in a mesh: prow: 8 (over z, core), pcol: 4 (over y, x).
Axes of the slice: x: 2, y: 2, z: 4, core: 2. Of those that a mesh axis runs over, the one named last changes fastest.
Arguments:
- tiles: bfloat16 [4096, 128, 128], P(('prow', 'pcol')), may hold values from -6 to 6
- tile_pos: int32 [4096, 2], P(('prow', 'pcol')), may hold values from -1 to 255, as said below
- pivots: int32 [2, 256], replicated, may hold values from 0 to 255, each once within a row
- inverses: bfloat16 [2, 256, 256], replicated, may hold values from -0.0234375 to 0.0234375
Outputs:
- factored: bfloat16 [4096, 128, 128], P(('prow', 'pcol'))
Inputs may be any that keep to these rules, and one draw needn't show every extreme that they name: `tile_pos`: slot s of device (p, q) (device index p * 4 + q, p along prow) holds a tile (I, J) with I % 8 == p and (J // 2) % 4 == q, or is empty; no tile is listed twice; every tile with I < 4 or J < 4 is listed; listed slots come before empty ones on each device; some device has all 128 slots listed.
All inputs are finite; a program needn't handle non-finite values.
Results may differ from a plain program's by a relative error of at most 0.0067.
Values may be sent and summed in bfloat16 or wider, within the bound.
A program may use at most 128 MiB of HBM per device.

v0:
```python
import jax
import jax.numpy as jnp
from jax import lax
from jax.sharding import PartitionSpec as P

ROW_TILES = 32


def broadcast(value, axis, root):
    mine = lax.axis_index(axis) == root
    return lax.psum(jnp.where(mine, value, jnp.zeros_like(value)), axis)


def slot_lookup(keys, count):
    targets = jnp.arange(count, dtype=jnp.int32)
    matches = keys[None, :] == targets[:, None]
    positions = jnp.arange(keys.shape[0], dtype=jnp.int32)
    chosen = jnp.sum(jnp.where(matches, positions[None, :], 0), axis=1)
    found = jnp.any(matches, axis=1)
    return (chosen, found)


def local(tiles, tile_pos, pivots, inverses):
    slots, edge, _ = tiles.shape
    row_procs = lax.axis_size("prow")
    col_procs = lax.axis_size("pcol")
    my_col = lax.axis_index("pcol")
    row_tiles = ROW_TILES
    col_tiles = ROW_TILES * row_procs // col_procs
    tile_row = tile_pos[:, 0]
    tile_col = tile_pos[:, 1]
    local_row = jnp.clip(tile_row // row_procs, 0, row_tiles - 1)
    local_col = jnp.clip(2 * (tile_col // 2 // col_procs) + tile_col % 2, 0, col_tiles - 1)
    nothing = jnp.zeros((), jnp.bfloat16)
    current = tiles
    for panel in range(2):
        first = 2 * panel
        in_column = (tile_col >= first) & (tile_col < first + 2)
        col_keys = jnp.where(in_column, local_row * 2 + tile_col - first, -1)
        chosen, found = slot_lookup(col_keys, 2 * row_tiles)
        column = jnp.where(found[:, None, None], current[chosen], nothing)
        column = (
            column.reshape(row_tiles, 2, edge, edge)
            .transpose(0, 2, 1, 3)
            .reshape(row_tiles * edge, 2 * edge)
        )
        inverse = inverses[panel]

        def multiply(block):
            return jnp.dot(block, inverse, preferred_element_type=jnp.float32).astype(jnp.bfloat16)

        def blank(block):
            return jnp.zeros(block.shape, jnp.bfloat16)

        lower = lax.cond(my_col == panel, multiply, blank, column)
        lower = broadcast(lower, "pcol", panel)
        in_block = (tile_row >= first) & (tile_row < first + 2)
        row_keys = jnp.where(in_block, local_col, -1)
        chosen, found = slot_lookup(row_keys, col_tiles)
        mine = jnp.where(found[:, None, None], current[chosen], nothing)
        mine = mine.transpose(1, 0, 2).reshape(edge, col_tiles * edge)
        order = pivots[panel]
        top_rows = broadcast(mine, "prow", first)
        bottom_rows = broadcast(mine, "prow", first + 1)
        upper = jnp.concatenate([top_rows, bottom_rows], axis=0)[order]
        lower_tiles = lower.reshape(row_tiles, edge, 2 * edge)
        upper_tiles = upper.reshape(2 * edge, col_tiles, edge).transpose(1, 0, 2)
        left = lower_tiles[local_row]
        right = upper_tiles[local_col]
        product = jnp.einsum("sik,skj->sij", left, right, preferred_element_type=jnp.float32)
        updated = (current.astype(jnp.float32) - product).astype(jnp.bfloat16)
        lower_parts = lower_tiles.reshape(row_tiles, edge, 2, edge).transpose(0, 2, 1, 3)
        lower_write = lower_parts[local_row, jnp.clip(tile_col - first, 0, 1)]
        upper_parts = upper_tiles.reshape(col_tiles, 2, edge, edge)
        upper_write = upper_parts[local_col, jnp.clip(tile_row - first, 0, 1)]
        trailing = (tile_row >= first + 2) & (tile_col >= first + 2)
        is_lower = in_column & (tile_row >= first + 2)
        current = jnp.where(trailing[:, None, None], updated, current)
        current = jnp.where(is_lower[:, None, None], lower_write, current)
        current = jnp.where(in_block[:, None, None], upper_write, current)
    return current


def solution(mesh):
    return jax.shard_map(
        local,
        mesh=mesh,
        in_specs=(P(("prow", "pcol"), None, None), P(("prow", "pcol"), None), P(), P()),
        out_specs=P(("prow", "pcol"), None, None),
        check_vma=False,
    )
```

profile of v0, /device:TPU:28, one launch (start us, length us, event | category | flops | bytes accessed | tf_op | source)
XLA Modules:
  0.0 487.1 jit_solution(5476775636218438579)
XLA Ops:
  6.5 0.8 add_select_fusion
  7.3 0.8 broadcast_select_fusion.4
  8.1 0.1 select_reduce_fusion.2
  8.2 0.1 fusion.15
  8.3 4.3 gather_fusion
  12.7 3.3 select_bitcast_fusion.5
  15.9 4.1 copy.34
  20.0 4.1 copy.35
  24.1 2.9 copy.36
  27.0 4.1 copy.37
  31.0 0.0 all-reduce.13.cloned.1.call-update
  31.1 0.0 all-reduce.7.cloned.1.call-start
  31.1 0.0 copy-start.2
  31.1 4.4 gather_fusion.3
  35.5 0.1 broadcast_in_dim.152
  35.6 1.8 select_bitcast_fusion.3
  37.4 0.2 conditional.2
  37.5 0.1 broadcast.543
  37.6 0.0 copy-start.3
  37.6 0.0 copy-start.4
  37.6 1.5 broadcast_select_fusion.3
  39.1 0.0 all-reduce.7.cloned.1.call-update
  39.1 0.3 all-reduce.11.cloned.1.call-start
  39.4 0.1 select_reduce_fusion
  39.5 0.1 fusion.14
  39.8 88.4 %all-reduce.13.cloned.1.call-done = (bf16[128,8192]{1,0:T(8,128)(2,1)}, bf16[128,8192]{1,0:T(8,128)(2,1)}) async-done(((bf16[128,8192]{1,0:T(8,128)(2,1)}, bf16[128,8192]{1,0:T(8,128)(2,1)}), (bf16[128,8192]{1,0:T(8,128)(2,1)}, bf16[128,8192]{1,0:T(8,128)(2,1)})) %all-reduce.13.cloned.1.call-update) | async-done | bytes 4194320 | tf_op jit(solution)/shard_map/psum | solution.py:11
  128.2 4.7 pad_maximum_fusion
  132.9 11.7 %gather_fusion.1 = bf16[256,8192]{1,0:T(8,128)(2,1)} fusion(bf16[256,8192]{1,0:T(8,128)(2,1)} %pad_maximum_fusion, s32[1024]{0:T(1024)S(1)} %pad_clamp_fusion.6), kind=kCustom, calls=%fused_computation.1 | custom fusion | bytes 8389632 | tf_op jit(solution)/shard_map/gather | solution.py:65
  144.5 7.7 %fusion.42 = (bf16[64,256,128]{2,1,0:T(8,128)(2,1)}, bf16[256,64,128]{2,0,1:T(8,128)(2,1)}) fusion(bf16[256,8192]{1,0:T(8,128)(2,1)} %gather_fusion.1), kind=kLoop, calls=%fused_computation.147 | loop fusion | bytes 12582912 | tf_op jit(solution)/shard_map/transpose | solution.py:67
  152.2 49.5 %all-reduce.7.cloned.1.call-done = bf16[4096,256]{1,0:T(8,128)(2,1)} async-done(((bf16[4096,256]{1,0:T(8,128)(2,1)}), bf16[4096,256]{1,0:T(8,128)(2,1)}) %all-reduce.7.cloned.1.call-update) | async-done | bytes 2097168 | tf_op jit(solution)/shard_map/psum | solution.py:11
  201.7 4.3 reshape.507
  206.1 3.5 copy.75
  209.5 8.8 %gather_fusion.6 = bf16[128,256,128]{2,1,0:T(8,128)(2,1)} fusion(bf16[64,256,128]{2,1,0:T(8,128)(2,1)} %get-tuple-element.55, s32[1024]{0:T(1024)S(1)} %pad_clamp_fusion.3), kind=kCustom, calls=%fused_computation.6 | custom fusion | bytes 16777728 | tf_op jit(solution)/shard_map/gather | solution.py:69
  218.3 5.3 %gather_fusion.2 = bf16[128,128,128]{2,1,0:T(8,128)(2,1)} fusion(bf16[64,2,128,128]{3,2,1,0:T(8,128)(2,1)} %bitcast.163, s32[128]{0:T(128)S(1)} %get-tuple-element.70), kind=kCustom, calls=%fused_computation.2 | custom fusion | bytes 8389632 | tf_op jit(solution)/shard_map/gather | solution.py:75
  223.6 4.8 gather_fusion.4
  228.4 6.6 %gather_fusion.5 = bf16[128,128,256]{2,1,0:T(8,128)(2,1)} fusion(bf16[32,128,256]{2,1,0:T(8,128)(2,1)S(1)} %bitcast.156, s32[1024]{0:T(1024)S(1)} %pad_clamp_fusion.4), kind=kCustom, calls=%fused_computation.5 | custom fusion | bytes 16777728 | tf_op jit(solution)/shard_map/gather | solution.py:68
  235.0 15.9 %fusion.13 = bf16[128,128,128]{2,1,0:T(8,128)(2,1)} fusion(bf16[128,128,128]{2,1,0:T(8,128)(2,1)} %gather_fusion.2, bf16[128,128,128]{2,1,0:T(8,128)(2,1)} %gather_fusion.4, bf16[128,128,128]{2,1,0:T(8,128)(2,1)} %param.8, pred[128]{0:T(512)(128)(4,1)S(1)} %get-tuple-element.67, pred[128]{0:T(512)(128)(4,1)S(1)} %get-tuple-element.68, ...), kind=kOutput, calls=%fused_computation.31 | convolution fusion | flops 1086324736 | bytes 33554816 | tf_op jit(solution)/shard_map/sik,skj->sij/dot_general | solution.py:70
  250.9 4.3 gather_fusion.7
  255.2 3.2 select_bitcast_fusion.2
  258.5 4.1 copy.42
  262.5 4.1 copy.43
  266.6 2.9 copy.44
  269.5 4.1 copy.45
  273.6 0.0 all-reduce.11.cloned.1.call-update
  273.6 0.0 all-reduce.9.cloned.1.call-start
  273.7 0.1 broadcast_in_dim.159
  273.8 4.3 gather_fusion.10
  278.1 1.9 select_bitcast_fusion
  280.0 0.3 conditional.3
  280.0 0.1 broadcast.544
  280.4 1.5 broadcast_select_fusion.2
  281.8 0.0 all-reduce.9.cloned.1.call-update
  281.9 88.1 %all-reduce.11.cloned.1.call-done = (bf16[128,8192]{1,0:T(8,128)(2,1)}, bf16[128,8192]{1,0:T(8,128)(2,1)}) async-done(((bf16[128,8192]{1,0:T(8,128)(2,1)}, bf16[128,8192]{1,0:T(8,128)(2,1)}), (bf16[128,8192]{1,0:T(8,128)(2,1)}, bf16[128,8192]{1,0:T(8,128)(2,1)})) %all-reduce.11.cloned.1.call-update) | async-done | bytes 4194320 | tf_op jit(solution)/shard_map/psum | solution.py:11
  369.9 4.6 pad_maximum_fusion.1
  374.5 11.7 %gather_fusion.8 = bf16[256,8192]{1,0:T(8,128)(2,1)} fusion(bf16[256,8192]{1,0:T(8,128)(2,1)} %pad_maximum_fusion.1, s32[1024]{0:T(1024)S(1)} %pad_clamp_fusion.1), kind=kCustom, calls=%fused_computation.8 | custom fusion | bytes 8389632 | tf_op jit(solution)/shard_map/gather | solution.py:65
  386.2 7.7 %fusion.43 = (bf16[64,256,128]{2,1,0:T(8,128)(2,1)}, bf16[256,64,128]{2,0,1:T(8,128)(2,1)}) fusion(bf16[256,8192]{1,0:T(8,128)(2,1)} %gather_fusion.8), kind=kLoop, calls=%fused_computation.148 | loop fusion | bytes 12582912 | tf_op jit(solution)/shard_map/transpose | solution.py:67
  393.9 9.0 %gather_fusion.13 = bf16[128,256,128]{2,1,0:T(8,128)(2,1)} fusion(bf16[64,256,128]{2,1,0:T(8,128)(2,1)} %get-tuple-element.53, s32[1024]{0:T(1024)S(1)} %pad_clamp_fusion.3), kind=kCustom, calls=%fused_computation.13 | custom fusion | bytes 16777728 | tf_op jit(solution)/shard_map/gather | solution.py:69
  402.9 40.8 %all-reduce.9.cloned.1.call-done = bf16[4096,256]{1,0:T(8,128)(2,1)} async-done(((bf16[4096,256]{1,0:T(8,128)(2,1)}), bf16[4096,256]{1,0:T(8,128)(2,1)}) %all-reduce.9.cloned.1.call-update) | async-done | bytes 2097168 | tf_op jit(solution)/shard_map/psum | solution.py:11
  443.7 8.3 %gather_fusion.12 = bf16[128,128,256]{2,1,0:T(8,128)(2,1)} fusion(bf16[32,128,256]{2,1,0:T(8,128)(2,1)} %bitcast.157, s32[1024]{0:T(1024)S(1)} %pad_clamp_fusion.4), kind=kCustom, calls=%fused_computation.12 | custom fusion | bytes 16777728 | tf_op jit(solution)/shard_map/gather | solution.py:68
  452.0 2.0 reshape.508
  454.0 2.1 copy.74
  456.2 5.3 %gather_fusion.9 = bf16[128,128,128]{2,1,0:T(8,128)(2,1)} fusion(bf16[64,2,128,128]{3,2,1,0:T(8,128)(2,1)} %bitcast.162, s32[128]{0:T(128)S(1)} %get-tuple-element.71), kind=kCustom, calls=%fused_computation.9 | custom fusion | bytes 8389632 | tf_op jit(solution)/shard_map/gather | solution.py:75
  461.4 3.1 gather_fusion.11
  464.5 15.8 %fusion.11 = bf16[128,128,128]{2,1,0:T(8,128)(2,1)} fusion(bf16[128,128,128]{2,1,0:T(8,128)(2,1)} %gather_fusion.9, bf16[128,128,128]{2,1,0:T(8,128)(2,1)} %gather_fusion.11, bf16[128,128,128]{2,1,0:T(8,128)(2,1)} %fusion.13, pred[128]{0:T(512)(128)(4,1)S(1)} %get-tuple-element.66, pred[128]{0:T(512)(128)(4,1)S(1)} %get-tuple-element.64, ...), kind=kOutput, calls=%fused_computation.29 | convolution fusion | flops 1086324736 | bytes 33554816 | tf_op jit(solution)/shard_map/sik,skj->sij/dot_general | solution.py:70
  (24 shorter events, 0.1 us)
Async XLA Ops:
  6.5 121.6 %all-reduce.13.cloned.1.call-start = ((), (), s32[]{:S(2)}) async-start(), calls=%async_computation.3 | async-start | bytes 8388608 | tf_op jit(solution)/shard_map/psum | solution.py:11
  31.1 170.7 %all-reduce.7.cloned.1.call-start = ((), (), s32[]{:S(2)}) async-start(), calls=%async_computation | async-start | bytes 4194304 | tf_op jit(solution)/shard_map/psum | solution.py:11
  31.1 6.3 %copy-start.2 = (bf16[2,256,256]{2,1,0:T(8,128)(2,1)S(1)}, bf16[2,256,256]{2,1,0:T(8,128)(2,1)}, u32[]{:S(2)}) copy-start(bf16[2,256,256]{2,1,0:T(8,128)(2,1)} %param.11) | copy-start | bytes 786436
  37.6 1.8 copy-start.3
  37.6 2.0 copy-start.4
  39.1 330.8 %all-reduce.11.cloned.1.call-start = ((), (), s32[]{:S(2)}) async-start(), calls=%async_computation.2 | async-start | bytes 8388608 | tf_op jit(solution)/shard_map/psum | solution.py:11
  223.6 4.8 copy-start
  273.6 170.0 %all-reduce.9.cloned.1.call-start = ((), (), s32[]{:S(2)}) async-start(), calls=%async_computation.1 | async-start | bytes 4194304 | tf_op jit(solution)/shard_map/psum | solution.py:11
  443.7 8.3 %copy-start.1 = (bf16[4096,256]{1,0:T(8,128)(2,1)S(1)}, bf16[4096,256]{1,0:T(8,128)(2,1)}, u32[]{:S(2)}) copy-start(bf16[4096,256]{1,0:T(8,128)(2,1)} %all-reduce.9.cloned.1.call-done) | copy-start | bytes 6291460
Sparse Core Ops, SparseCore 0:
  31.2 96.9 all-reduce.12
  131.3 70.4 all-reduce.6
  273.8 96.1 all-reduce.10
  373.2 70.4 all-reduce.8
where the time goes:
time: 495 us; the launch traced here: 487 us
  waiting for transfers between devices  267 us (54%)
  local copies, waits for them, and re-layouts  150 us (30%)
  matrix products  31.7 us (6%)
  other arithmetic  24.5 us (5%)
  between operations  13.6 us (3%)
    psum x4, waiting for transfers between devices, broadcast(): return lax.psum(jnp.where(mine, value, jnp.zeros_like(value)), axis)  267 us
    dot_general x2, matrix products, local(): jnp.einsum('sik,skj->sij', left, right, preferred_element_type=jnp.float32)  31.7 us
    select_n x8, local copies, waits for them, and re-layouts, broadcast(): return lax.psum(jnp.where(mine, value, jnp.zeros_like(value)), axis)  30.3 us
    gather x2, local copies, waits for them, and re-layouts, local(): upper = jnp.concatenate([top_rows, bottom_rows], axis=0)[order]  23.3 us
    gather x2, local copies, waits for them, and re-layouts, local(): right = upper_tiles[local_col]  17.7 us
    transpose x2, local copies, waits for them, and re-layouts, local(): upper_tiles = upper.reshape(2 * edge, col_tiles, edge).transpose(1, 0, 2)  15.4 us
    gather x2, local copies, waits for them, and re-layouts, local(): left = lower_tiles[local_row]  14.9 us
    another operation x4, local copies, waits for them, and re-layouts, local(): lower_tiles.reshape(row_tiles, edge, 2, edge).transpose(0, 2, 1, 3)  11.9 us
  transfers between devices with their start and end apart: 4, of which 4 were waited for; matrix products, arithmetic and copies ran while one was open for 15% of the time, Pallas kernels for 0%

commit v1 on v0

v1 whole, which is shorter than its diff:
```python
import functools
import jax
import jax.numpy as jnp
from jax import lax
from jax.experimental import pallas as pl
from jax.experimental.pallas import tpu as pltpu
from jax.sharding import PartitionSpec as P

ROW_TILES = 32
CHUNKS = 16
GROUP = 8
MESH = pl.DeviceIdType.MESH


def slot_lookup(keys, count):
    targets = jnp.arange(count, dtype=jnp.int32)
    matches = keys[None, :] == targets[:, None]
    positions = jnp.arange(keys.shape[0], dtype=jnp.int32)
    return jnp.sum(jnp.where(matches, positions[None, :], 0), axis=1)


def exchange(
    nz, nbits, cols,
    slot_r, slot_l, tiles,
    rows, side, ext_r, ext_c,
    up_send, down_send, sib_send, z_recv, sib_recv,
    l_send, l_recv, e_sem, f_send, f_recv,
):
    p = lax.axis_index("prow")
    v = lax.axis_index("pcol")
    z = p // 2
    core = p % 2
    other = p + 1 - 2 * core
    cw = cols // CHUNKS
    rw = ROW_TILES // CHUNKS
    n = CHUNKS

    def flip(b):
        return v + b - 2 * b * ((v // b) % 2)

    barrier = pltpu.get_barrier_semaphore()

    @pl.when(z > 0)
    def _():
        pl.semaphore_signal(barrier, inc=1, device_id={"prow": p - 2, "pcol": v}, device_id_type=MESH)

    @pl.when(z < nz - 1)
    def _():
        pl.semaphore_signal(barrier, inc=1, device_id={"prow": p + 2, "pcol": v}, device_id_type=MESH)

    pl.semaphore_signal(barrier, inc=1, device_id={"prow": other, "pcol": v}, device_id_type=MESH)
    for bi in range(nbits):
        pl.semaphore_signal(barrier, inc=1, device_id={"prow": p, "pcol": flip(1 << bi)}, device_id_type=MESH)

    @pl.when(z < 2)
    def _():
        @pl.loop(0, cols)
        def _(c):
            rows[c, p] = tiles[slot_r[c]]

    @pl.when(v < 2)
    def _():
        @pl.loop(0, ROW_TILES)
        def _(i):
            side[v, i, 0] = tiles[slot_l[2 * i]]
            side[v, i, 1] = tiles[slot_l[2 * i + 1]]

    ends = (z == 0).astype(jnp.int32) + (z == nz - 1).astype(jnp.int32)
    pl.semaphore_wait(barrier, 3 + nbits - ends)

    def block(k, j):
        return rows.at[pl.ds(j * cw, cw), 2 * k + core]

    def up(k, j):
        return pltpu.make_async_remote_copy(
            block(k, j), block(k, j), up_send.at[k, j], z_recv.at[k, j],
            device_id={"prow": p + 2, "pcol": v}, device_id_type=MESH)

    def down(k, j):
        return pltpu.make_async_remote_copy(
            block(k, j), block(k, j), down_send.at[k, j], z_recv.at[k, j],
            device_id={"prow": p - 2, "pcol": v}, device_id_type=MESH)

    def sib(k, j):
        return pltpu.make_async_remote_copy(
            block(k, j), block(k, j), sib_send.at[k, j], sib_recv.at[k, j],
            device_id={"prow": other, "pcol": v}, device_id_type=MESH)

    def sib_in(k, j):
        there = rows.at[pl.ds(j * cw, cw), 2 * k + 1 - core]
        return pltpu.make_async_remote_copy(
            there, there, sib_send.at[k, j], sib_recv.at[k, j],
            device_id={"prow": other, "pcol": v}, device_id_type=MESH)

    def goes_up(k):
        return jnp.logical_and(z >= k, z < nz - 1)

    def goes_down(k):
        return jnp.logical_and(z <= k, z > 0)

    def forward(k, j):
        @pl.when(goes_up(k))
        def _():
            up(k, j).start()

        @pl.when(goes_down(k))
        def _():
            down(k, j).start()

        sib(k, j).start()

    def own(k, j):
        @pl.when(z == k)
        def _():
            forward(k, j)

    def label(s):
        return v if s == 0 else v + 1 - 2 * (v % 2)

    def side_copy(s, j, bi):
        part = side.at[s, pl.ds(j * rw, rw)]
        return pltpu.make_async_remote_copy(
            part, part, l_send.at[s, bi, j], l_recv.at[s, j],
            device_id={"prow": p, "pcol": flip(1 << bi)}, device_id_type=MESH)

    def side_forward(s, j):
        for bi in range(nbits):
            @pl.when(label(s) % (2 << bi) == 0)
            def _():
                side_copy(s, j, bi).start()

    def ext_copy(source, sem, target, recv):
        return pltpu.make_async_remote_copy(
            source, ext_r.at[core], e_sem.at[sem], e_sem.at[recv],
            device_id={"prow": target, "pcol": v}, device_id_type=MESH)

    def ext_forward(source):
        @pl.when(goes_up(1))
        def _():
            ext_copy(source, 0, p + 2, 3).start()

        @pl.when(goes_down(1))
        def _():
            ext_copy(source, 1, p - 2, 3).start()

        ext_copy(source, 2, other, 4).start()

    def corner_copy(source, bi):
        return pltpu.make_async_remote_copy(
            source, ext_c, f_send.at[bi], f_recv.at[0],
            device_id={"prow": p, "pcol": flip(1 << bi)}, device_id_type=MESH)

    def corner_forward(source):
        for bi in range(nbits):
            @pl.when(label(1) % (2 << bi) == 0)
            def _():
                corner_copy(source, bi).start()

    for k in range(2):
        own(k, 0)
        own(k, 1)

    @pl.loop(0, n)
    def _(j):
        @pl.when(j + 2 < n)
        def _():
            own(0, j + 2)
            own(1, j + 2)

        @pl.when(j < n // 2)
        def _():
            for h in range(2):
                for s in range(2):
                    @pl.when(v == s)
                    def _():
                        side_forward(s, 2 * j + h)

        for k in (1, 0):
            @pl.when(z != k)
            def _():
                up(k, j).wait_recv()
                forward(k, j)

        @pl.when(j < n // 2)
        def _():
            for h in range(2):
                for s in range(2):
                    @pl.when(v != s)
                    def _():
                        side_copy(s, 2 * j + h, 0).wait_recv()
                        side_forward(s, 2 * j + h)

        @pl.when(jnp.logical_and(j == 0, z == 1))
        def _():
            ext_forward(side.at[0, 0])
            ext_r[core] = side[0, 0]

        @pl.when(jnp.logical_and(j == 2, z != 1))
        def _():
            ext_copy(ext_r.at[core], 0, other, 3).wait_recv()
            ext_forward(ext_r.at[core])

        @pl.when(j == 2)
        def _():
            sib_in(0, 0).wait_recv()

            @pl.when(v == 1)
            def _():
                corner_forward(rows.at[pl.ds(0, 2), pl.ds(0, 2)])
                ext_c[...] = rows[pl.ds(0, 2), pl.ds(0, 2)]

        @pl.when(jnp.logical_and(j == 4, v != 1))
        def _():
            corner_copy(ext_c, 0).wait_recv()
            corner_forward(ext_c)

    @pl.loop(0, n)
    def _(j):
        for k in range(2):
            @pl.when(goes_up(k))
            def _():
                up(k, j).wait_send()

            @pl.when(goes_down(k))
            def _():
                down(k, j).wait_send()

            sib(k, j).wait_send()

        sib_in(1, j).wait_recv()

        @pl.when(j > 0)
        def _():
            sib_in(0, j).wait_recv()

        for s in range(2):
            for bi in range(nbits):
                @pl.when(label(s) % (2 << bi) == 0)
                def _():
                    side_copy(s, j, bi).wait_send()

    @pl.when(goes_up(1))
    def _():
        ext_copy(ext_r.at[core], 0, other, 3).wait_send()

    @pl.when(goes_down(1))
    def _():
        ext_copy(ext_r.at[core], 1, other, 3).wait_send()

    ext_copy(ext_r.at[core], 2, other, 4).wait_send()
    pltpu.make_async_remote_copy(
        ext_r.at[core], ext_r.at[1 - core], e_sem.at[2], e_sem.at[4],
        device_id={"prow": other, "pcol": v}, device_id_type=MESH).wait_recv()
    for bi in range(nbits):
        @pl.when(label(1) % (2 << bi) == 0)
        def _():
            corner_copy(ext_c, bi).wait_send()


def dot(a, b):
    return jnp.dot(a, b, preferred_element_type=jnp.float32)


def update(
    cols, place,
    order, inverse, rows, side, ext_r, ext_c, tiles,
    out,
    m0, m1, r1, final,
):
    p = lax.axis_index("prow")
    v = lax.axis_index("pcol")
    bf = jnp.bfloat16
    spread = lax.broadcasted_iota(jnp.int32, (256, 256), 1)
    perm0 = (order[0] == spread).astype(bf)
    perm1 = (order[1] == spread).astype(bf)
    inv0, inv1 = inverse[0], inverse[1]
    mix0 = dot(inv0, perm0).astype(bf)
    mix1 = dot(inv1, perm1).astype(bf)
    corner = jnp.concatenate(
        [jnp.concatenate([ext_c[0, r], ext_c[1, r]], axis=1) for r in range(2)], axis=0)
    pivot_rows = jnp.concatenate(
        [jnp.concatenate([ext_r[r, 0], ext_r[r, 1]], axis=1) for r in range(2)], axis=0)
    step = 4

    @pl.loop(0, ROW_TILES, step=step)
    def _(i):
        def wide(s):
            return jnp.concatenate(
                [side[s, pl.ds(i, step), h].reshape(step * 128, 128) for h in range(2)], axis=1)

        left = wide(0)
        lower = dot(left, mix0).astype(bf)
        m0[pl.ds(i, step)] = lower.reshape(step, 128, 256)
        right = (wide(1).astype(jnp.float32) - dot(lower, corner)).astype(bf)
        m1[pl.ds(i, step)] = dot(right, mix1).astype(bf).reshape(step, 128, 256)

        def keep(value):
            for u in range(step):
                for h in range(2):
                    final[cols + 2 * (i + u) + h] = value[u * 128:(u + 1) * 128, h * 128:(h + 1) * 128]

        @pl.when(v == 0)
        def _():
            keep(dot(left, inv0).astype(bf))

        @pl.when(v == 1)
        def _():
            keep(dot(right, inv1).astype(bf))

    lead = dot(pivot_rows, mix0).astype(bf)

    @pl.loop(0, cols, step=step)
    def _(c):
        top = jnp.concatenate([rows[c + u, pl.ds(0, 2)].reshape(256, 128) for u in range(step)], axis=1)
        low = jnp.concatenate([rows[c + u, pl.ds(2, 2)].reshape(256, 128) for u in range(step)], axis=1)
        value = (low.astype(jnp.float32) - dot(lead, top)).astype(bf)
        for u in range(step):
            r1[c + u] = value[:, u * 128:(u + 1) * 128]

    @pl.when(v == 0)
    def _():
        value = dot(pivot_rows, inv0).astype(bf)
        r1[0] = value[:, :128]
        r1[1] = value[:, 128:]

    narrow = lax.broadcasted_iota(jnp.int32, (128, 256), 1)

    @pl.when(p < 2)
    def _():
        part = (order[0, pl.ds(p * 128, 128)] == narrow).astype(bf)

        @pl.loop(0, cols, step=step)
        def _(c):
            top = jnp.concatenate([rows[c + u, pl.ds(0, 2)].reshape(256, 128) for u in range(step)], axis=1)
            value = dot(part, top).astype(bf)
            for u in range(step):
                final[c + u] = value[:, u * 128:(u + 1) * 128]

    @pl.when(jnp.logical_and(p >= 2, p < 4))
    def _():
        part = (order[1, pl.ds((p - 2) * 128, 128)] == narrow).astype(bf)

        @pl.loop(0, cols, step=step)
        def _(c):
            low = jnp.concatenate([r1[c + u] for u in range(step)], axis=1)
            value = dot(part, low).astype(bf)
            for u in range(step):
                final[c + u] = value[:, u * 128:(u + 1) * 128]

    slots = tiles.shape[0]

    @pl.loop(0, slots, step=GROUP)
    def _(base):
        for u in range(GROUP):
            s = base + u
            i, c, f, kind = place[0, s], place[1, s], place[2, s], place[3, s]
            old = tiles[s].astype(jnp.float32)
            total = dot(m0[i], rows[c, pl.ds(0, 2)].reshape(256, 128)) + dot(m1[i], r1[c])
            other = jnp.where(kind == 1, final[f].astype(jnp.float32), old)
            out[s] = jnp.where(kind == 0, old - total, other).astype(bf)


def local(tiles, tile_pos, pivots, inverses):
    slots, edge, _ = tiles.shape
    row_procs = lax.axis_size("prow")
    col_procs = lax.axis_size("pcol")
    nz = row_procs // 2
    nbits = col_procs.bit_length() - 1
    cols = ROW_TILES * row_procs // col_procs
    tile_row = tile_pos[:, 0]
    tile_col = tile_pos[:, 1]
    local_row = jnp.clip(tile_row // row_procs, 0, ROW_TILES - 1)
    local_col = jnp.clip(2 * (tile_col // 2 // col_procs) + tile_col % 2, 0, cols - 1)
    listed = tile_row >= 0
    is_upper = listed & (tile_row < 4)
    is_side = listed & (tile_col < 4)
    side_key = local_row * 2 + tile_col % 2
    slot_r = slot_lookup(jnp.where(is_upper, local_col, -1), cols)
    slot_l = slot_lookup(jnp.where(is_side, side_key, -1), 2 * ROW_TILES)
    done = jnp.where(is_upper, local_col, cols + side_key)
    kind = jnp.where(listed, jnp.where(is_upper | is_side, 1, 0), 2)
    done = jnp.where(kind == 1, done, 0)
    place = jnp.stack([local_row, local_col, done, kind]).astype(jnp.int32)

    bf = jnp.bfloat16
    smem = pl.BlockSpec(memory_space=pltpu.SMEM)
    vmem = pl.BlockSpec(memory_space=pltpu.VMEM)
    dma = pltpu.SemaphoreType.DMA
    n = CHUNKS
    rows, side, ext_r, ext_c = pl.pallas_call(
        functools.partial(exchange, nz, nbits, cols),
        out_shape=[
            jax.ShapeDtypeStruct((cols, 4, edge, edge), bf),
            jax.ShapeDtypeStruct((2, ROW_TILES, 2, edge, edge), bf),
            jax.ShapeDtypeStruct((2, 2, edge, edge), bf),
            jax.ShapeDtypeStruct((2, 2, edge, edge), bf),
        ],
        in_specs=[smem, smem, vmem],
        out_specs=[vmem] * 4,
        scratch_shapes=[
            dma((2, n)), dma((2, n)), dma((2, n)), dma((2, n)), dma((2, n)),
            dma((2, nbits, n)), dma((2, n)), dma((5,)), dma((nbits,)), dma((1,)),
        ],
        compiler_params=pltpu.CompilerParams(
            collective_id=0, has_side_effects=True, vmem_limit_bytes=40 * 1024 * 1024),
        name="exchange",
    )(slot_r, slot_l, tiles)
    return pl.pallas_call(
        functools.partial(update, cols),
        out_shape=jax.ShapeDtypeStruct(tiles.shape, bf),
        in_specs=[smem] + [vmem] * 7,
        out_specs=vmem,
        scratch_shapes=[
            pltpu.VMEM((ROW_TILES, edge, 2 * edge), bf),
            pltpu.VMEM((ROW_TILES, edge, 2 * edge), bf),
            pltpu.VMEM((cols, 2 * edge, edge), bf),
            pltpu.VMEM((cols + 2 * ROW_TILES, edge, edge), bf),
        ],
        compiler_params=pltpu.CompilerParams(vmem_limit_bytes=48 * 1024 * 1024),
        name="update",
    )(place, pivots.reshape(2, 2 * edge, 1), inverses, rows, side, ext_r, ext_c, tiles)


def solution(mesh):
    return jax.shard_map(
        local,
        mesh=mesh,
        in_specs=(P(("prow", "pcol"), None, None), P(("prow", "pcol"), None), P(), P()),
        out_specs=P(("prow", "pcol"), None, None),
        check_vma=False,
    )
```

time: 495 us -> 211 us (0.43); the launches traced: 487 us -> 211 us
  waiting for transfers between devices: 267 us -> 0 us
  Pallas kernels: 0 us -> 206 us
  local copies, waits for them, and re-layouts: 150 us -> 3.01 us
  matrix products: 31.7 us -> 0 us
  other arithmetic: 24.5 us -> 1.68 us
  between operations: 13.6 us -> 0.04 us
    psum x4 -> x0, waiting for transfers between devices: 267 us -> none  [broadcast(): return lax.psum(jnp.where(mine, value, jnp.zeros_like(value)), axis)]
    pallas_call x0 -> x2, Pallas kernels: none -> 206 us  [the longest x1 184 us: local(): pl.pallas_call(functools.partial(exchange, nz, nbits, cols), out_shape=[j...]
    gather x14 -> x0, local copies, waits for them, and re-layouts: 91.8 us -> none  [the longest x2 23.3 us: local(): upper = jnp.concatenate([top_rows, bottom_rows], axis=0)[order]]
    dot_general x2 -> x0, matrix products: 31.7 us -> none  [local(): jnp.einsum('sik,skj->sij', left, right, preferred_element_type=jnp.float32)]
    select_n x8 -> x0, local copies, waits for them, and re-layouts: 30.3 us -> none  [broadcast(): return lax.psum(jnp.where(mine, value, jnp.zeros_like(value)), axis)]
    transpose x2 -> x0, local copies, waits for them, and re-layouts: 15.4 us -> none  [local(): upper_tiles = upper.reshape(2 * edge, col_tiles, edge).transpose(1, 0, 2)]
    another operation x6 -> x0, local copies, waits for them, and re-layouts: 12.2 us -> none  [the longest x4 11.9 us: local(): lower_tiles.reshape(row_tiles, edge, 2, edge).transpose(0, 2, 1, 3)]
    select_n x11 -> x2, other arithmetic: 11 us -> 1.56 us  [the longest x1 0.79 us: local(): done = jnp.where(kind == 1, done, 0)]
  transfers between devices with their start and end apart: 4 -> 0, of which waited for: 4 -> 0; matrix products, arithmetic and copies ran while one was open for 15% -> 0% of each run, Pallas kernels for 0% -> 0%
where the time goes in v1:
time: 211 us
  Pallas kernels  206 us (98%)
  local copies, waits for them, and re-layouts  3.01 us (1%)
    pallas_call x1, Pallas kernels, local(): pl.pallas_call(functools.partial(exchange, nz, nbits, cols), out_shape=[j...  184 us
    pallas_call x1, Pallas kernels, local(): pl.pallas_call(functools.partial(update, cols), out_shape=jax.ShapeDtypeS...  22.1 us

profile of v1, /device:TPU:28, one launch (start us, length us, event | category | flops | bytes accessed | tf_op | source)
XLA Modules:
  0.0 210.6 jit_solution(12006952182892830401)
XLA Ops:
  0.0 0.0 copy-start.1
  0.0 0.8 and_select_fusion.1
  0.8 0.1 select_reduce_fusion
  0.9 0.8 compare_select_fusion
  1.7 0.8 copy.6.order
  2.5 0.0 copy-start
  2.5 2.2 %copy-done = bf16[128,128,128]{2,1,0:T(8,128)(2,1)S(1)} copy-done((bf16[128,128,128]{2,1,0:T(8,128)(2,1)S(1)}, bf16[128,128,128]{2,1,0:T(8,128)(2,1)}, u32[]{:S(2)}) %copy-start) | copy-done | bytes 4194328
  4.7 183.8 %exchange.1 = (bf16[64,4,128,128]{3,2,1,0:T(8,128)(2,1)}, bf16[2,32,2,128,128]{4,3,2,1,0:T(8,128)(2,1)S(1)}, bf16[2,2,128,128]{3,2,1,0:T(8,128)(2,1)S(1)}, bf16[2,2,128,128]{3,2,1,0:T(8,128)(2,1)S(1)}) custom-call(s32[64]{0:T(128)S(1)} %get-tuple-element.20.slot_r, s32[64]{0:T(128)S(1)} %get-tuple-element.19.slot_l, bf16[128,128,128]{2,1,0:T(8,128)(2,1)S(1)} %copy-done), custom_call_target="tpu_custom_call" | custom-call | tf_op jit(solution)/shard_map/exchange/pallas_call | solution.py:390
  188.5 0.0 copy-done.1
  188.5 22.1 %update.1 = bf16[128,128,128]{2,1,0:T(8,128)(2,1)} custom-call(s32[4,128]{1,0:T(4,128)S(1)} %pad_add_fusion.place, s32[2,256,1]{2,1,0:T(8,128)S(1)} %copy.6.order, bf16[2,256,256]{2,1,0:T(8,128)(2,1)S(1)} %copy-done.1, bf16[64,4,128,128]{3,2,1,0:T(8,128)(2,1)} %get-tuple-element.9.rows, bf16[2,32,2,128,128]{4,3,2,1,0:T(8,128)(2,1)S(1)} %get-tuple-element.10.side, ...), custom_call_target="tpu_custom_call" | custom-call | tf_op jit(solution)/shard_map/update/pallas_call | solution.py:408
  (1 shorter events, 0.0 us)
Async XLA Ops:
  0.0 188.5 %copy-start.1 = (bf16[2,256,256]{2,1,0:T(8,128)(2,1)S(1)}, bf16[2,256,256]{2,1,0:T(8,128)(2,1)}, u32[]{:S(2)}) copy-start(bf16[2,256,256]{2,1,0:T(8,128)(2,1)} %inverse.1) | copy-start | bytes 786436
  2.5 2.2 %copy-start = (bf16[128,128,128]{2,1,0:T(8,128)(2,1)S(1)}, bf16[128,128,128]{2,1,0:T(8,128)(2,1)}, u32[]{:S(2)}) copy-start(bf16[128,128,128]{2,1,0:T(8,128)(2,1)} %tiles.3) | copy-start | bytes 12582916

commit v2 on v1

--- a/solution.py
+++ b/solution.py
@@ -156,6 +156,15 @@
             def _():
                 corner_copy(source, bi).start()
 
+    def side_turn(s, j):
+        depth = sum((label(s) // (1 << bi)) % 2 for bi in range(nbits))
+        at = j - 2 * depth + 1
+
+        @pl.when(jnp.logical_and(depth > 0, jnp.logical_and(at >= 0, at < n)))
+        def _():
+            side_copy(s, at, 0).wait_recv()
+            side_forward(s, at)
+
     for k in range(2):
         own(k, 0)
         own(k, 1)
@@ -167,13 +176,10 @@
             own(0, j + 2)
             own(1, j + 2)
 
-        @pl.when(j < n // 2)
-        def _():
-            for h in range(2):
-                for s in range(2):
-                    @pl.when(v == s)
-                    def _():
-                        side_forward(s, 2 * j + h)
+        for s in range(2):
+            @pl.when(v == s)
+            def _():
+                side_forward(s, j)
 
         for k in (1, 0):
             @pl.when(z != k)
@@ -181,21 +187,15 @@
                 up(k, j).wait_recv()
                 forward(k, j)
 
-        @pl.when(j < n // 2)
-        def _():
-            for h in range(2):
-                for s in range(2):
-                    @pl.when(v != s)
-                    def _():
-                        side_copy(s, 2 * j + h, 0).wait_recv()
-                        side_forward(s, 2 * j + h)
-
-        @pl.when(jnp.logical_and(j == 0, z == 1))
+        for s in range(2):
+            side_turn(s, j)
+
+        @pl.when(jnp.logical_and(j == 2 * nbits, z == 1))
         def _():
             ext_forward(side.at[0, 0])
             ext_r[core] = side[0, 0]
 
-        @pl.when(jnp.logical_and(j == 2, z != 1))
+        @pl.when(jnp.logical_and(j == 2 * nbits + 1, z != 1))
         def _():
             ext_copy(ext_r.at[core], 0, other, 3).wait_recv()
             ext_forward(ext_r.at[core])
@@ -213,6 +213,11 @@
         def _():
             corner_copy(ext_c, 0).wait_recv()
             corner_forward(ext_c)
+
+    @pl.loop(n, n + 2 * nbits)
+    def _(j):
+        for s in range(2):
+            side_turn(s, j)
 
     @pl.loop(0, n)
     def _(j):

time: 211 us -> 145 us (0.69)
  Pallas kernels: 206 us -> 140 us
    pallas_call x1, Pallas kernels: 184 us -> 118 us  [local(): pl.pallas_call(functools.partial(exchange, nz, nbits, cols), out_shape=[j...]
where the time goes in v2:
time: 145 us
  Pallas kernels  140 us (97%)
  local copies, waits for them, and re-layouts  3.01 us (2%)
  other arithmetic  1.68 us (1%)
    pallas_call x1, Pallas kernels, local(): pl.pallas_call(functools.partial(exchange, nz, nbits, cols), out_shape=[j...  118 us
    pallas_call x1, Pallas kernels, local(): pl.pallas_call(functools.partial(update, cols), out_shape=jax.ShapeDtypeS...  22.1 us

profile of v2, /device:TPU:28, one launch (start us, length us, event | category | flops | bytes accessed | tf_op | source)
XLA Modules:
  0.0 144.9 jit_solution(2767612000768547078)
XLA Ops:
  0.0 0.0 copy-start.1
  0.0 0.8 and_select_fusion.1
  0.8 0.1 select_reduce_fusion
  0.9 0.8 compare_select_fusion
  1.7 0.8 copy.6.order
  2.5 0.0 copy-start
  2.5 2.2 %copy-done = bf16[128,128,128]{2,1,0:T(8,128)(2,1)S(1)} copy-done((bf16[128,128,128]{2,1,0:T(8,128)(2,1)S(1)}, bf16[128,128,128]{2,1,0:T(8,128)(2,1)}, u32[]{:S(2)}) %copy-start) | copy-done | bytes 4194328
  4.7 118.1 %exchange.1 = (bf16[64,4,128,128]{3,2,1,0:T(8,128)(2,1)}, bf16[2,32,2,128,128]{4,3,2,1,0:T(8,128)(2,1)S(1)}, bf16[2,2,128,128]{3,2,1,0:T(8,128)(2,1)S(1)}, bf16[2,2,128,128]{3,2,1,0:T(8,128)(2,1)S(1)}) custom-call(s32[64]{0:T(128)S(1)} %get-tuple-element.20.slot_r, s32[64]{0:T(128)S(1)} %get-tuple-element.19.slot_l, bf16[128,128,128]{2,1,0:T(8,128)(2,1)S(1)} %copy-done), custom_call_target="tpu_custom_call" | custom-call | tf_op jit(solution)/shard_map/exchange/pallas_call | solution.py:395
  122.8 0.0 copy-done.1
  122.8 22.1 %update.1 = bf16[128,128,128]{2,1,0:T(8,128)(2,1)} custom-call(s32[4,128]{1,0:T(4,128)S(1)} %pad_add_fusion.place, s32[2,256,1]{2,1,0:T(8,128)S(1)} %copy.6.order, bf16[2,256,256]{2,1,0:T(8,128)(2,1)S(1)} %copy-done.1, bf16[64,4,128,128]{3,2,1,0:T(8,128)(2,1)} %get-tuple-element.9.rows, bf16[2,32,2,128,128]{4,3,2,1,0:T(8,128)(2,1)S(1)} %get-tuple-element.10.side, ...), custom_call_target="tpu_custom_call" | custom-call | tf_op jit(solution)/shard_map/update/pallas_call | solution.py:413
  (1 shorter events, 0.0 us)
Async XLA Ops:
  0.0 122.8 %copy-start.1 = (bf16[2,256,256]{2,1,0:T(8,128)(2,1)S(1)}, bf16[2,256,256]{2,1,0:T(8,128)(2,1)}, u32[]{:S(2)}) copy-start(bf16[2,256,256]{2,1,0:T(8,128)(2,1)} %inverse.1) | copy-start | bytes 786436
  2.5 2.2 %copy-start = (bf16[128,128,128]{2,1,0:T(8,128)(2,1)S(1)}, bf16[128,128,128]{2,1,0:T(8,128)(2,1)}, u32[]{:S(2)}) copy-start(bf16[128,128,128]{2,1,0:T(8,128)(2,1)} %tiles.3) | copy-start | bytes 12582916

commit v3 on v2

--- a/solution.py
+++ b/solution.py
@@ -7,7 +7,8 @@
 from jax.sharding import PartitionSpec as P
 
 ROW_TILES = 32
-CHUNKS = 16
+CHUNKS = 32
+AHEAD = 3
 GROUP = 8
 MESH = pl.DeviceIdType.MESH
 
@@ -21,8 +22,9 @@
 
 def exchange(
     nz, nbits, cols,
-    slot_r, slot_l, tiles,
-    rows, side, ext_r, ext_c,
+    slot_r, slot_l, place, order, inverse, tiles,
+    out,
+    rows, side, ext_r, ext_c, m0, m1, r1, final, mixed, lead,
     up_send, down_send, sib_send, z_recv, sib_recv,
     l_send, l_recv, e_sem, f_send, f_recv,
 ):
@@ -34,6 +36,12 @@
     cw = cols // CHUNKS
     rw = ROW_TILES // CHUNKS
     n = CHUNKS
+    step = 4
+    per = step // cw
+    side_lag = 4 * ((2 * nbits + 6) // 4)
+    row_lag = 4 * ((2 * nbits + 2 * nz + 1) // 4)
+    panels = Panels(cols, order, inverse, rows, side, ext_r, ext_c, tiles, out, m0, m1, r1, final, place)
+    panels.lead = lead
 
     def flip(b):
         return v + b - 2 * b * ((v // b) % 2)
@@ -65,6 +73,7 @@
             side[v, i, 0] = tiles[slot_l[2 * i]]
             side[v, i, 1] = tiles[slot_l[2 * i + 1]]
 
+    panels.prepare(mixed)
     ends = (z == 0).astype(jnp.int32) + (z == nz - 1).astype(jnp.int32)
     pl.semaphore_wait(barrier, 3 + nbits - ends)
 
@@ -156,8 +165,38 @@
             def _():
                 corner_copy(source, bi).start()
 
+    def depth_of(s):
+        return sum((label(s) // (1 << bi)) % 2 for bi in range(nbits))
+
+    def compute(j):
+        at = j - side_lag
+
+        @pl.when(jnp.logical_and(at >= 0, jnp.logical_and(at < n, at % (step // rw) == 0)))
+        def _():
+            panels.side_step(at * rw, step)
+
+        @pl.when(j == row_lag)
+        def _():
+            pltpu.make_async_remote_copy(
+                ext_r.at[core], ext_r.at[1 - core], e_sem.at[2], e_sem.at[4],
+                device_id={"prow": other, "pcol": v}, device_id_type=MESH).wait_recv()
+            panels.set_lead()
+
+        first = j - row_lag
+
+        @pl.when(jnp.logical_and(first >= 0, jnp.logical_and(first < n, first % per == 0)))
+        def _():
+            for h in range(per):
+                sib_in(1, first + h).wait_recv()
+
+                @pl.when(jnp.logical_or(v != 1, (first + h) * cw >= 2))
+                def _():
+                    sib_in(0, first + h).wait_recv()
+
+            panels.row_step(first * cw, step)
+
     def side_turn(s, j):
-        depth = sum((label(s) // (1 << bi)) % 2 for bi in range(nbits))
+        depth = depth_of(s)
         at = j - 2 * depth + 1
 
         @pl.when(jnp.logical_and(depth > 0, jnp.logical_and(at >= 0, at < n)))
@@ -166,15 +205,15 @@
             side_forward(s, at)
 
     for k in range(2):
-        own(k, 0)
-        own(k, 1)
+        for j in range(AHEAD):
+            own(k, j)
 
     @pl.loop(0, n)
     def _(j):
-        @pl.when(j + 2 < n)
-        def _():
-            own(0, j + 2)
-            own(1, j + 2)
+        @pl.when(j + AHEAD < n)
+        def _():
+            own(0, j + AHEAD)
+            own(1, j + AHEAD)
 
         for s in range(2):
             @pl.when(v == s)
@@ -195,29 +234,35 @@
             ext_forward(side.at[0, 0])
             ext_r[core] = side[0, 0]
 
-        @pl.when(jnp.logical_and(j == 2 * nbits + 1, z != 1))
+        far = jnp.where(z == 0, 1, z - 1)
+
+        @pl.when(jnp.logical_and(j == 2 * nbits + 2 * far, z != 1))
         def _():
             ext_copy(ext_r.at[core], 0, other, 3).wait_recv()
             ext_forward(ext_r.at[core])
 
-        @pl.when(j == 2)
-        def _():
-            sib_in(0, 0).wait_recv()
-
-            @pl.when(v == 1)
-            def _():
-                corner_forward(rows.at[pl.ds(0, 2), pl.ds(0, 2)])
-                ext_c[...] = rows[pl.ds(0, 2), pl.ds(0, 2)]
-
-        @pl.when(jnp.logical_and(j == 4, v != 1))
+        @pl.when(jnp.logical_and(j == 4, v == 1))
+        def _():
+            for h in range(2 // min(cw, 2)):
+                sib_in(0, h).wait_recv()
+            corner_forward(rows.at[pl.ds(0, 2), pl.ds(0, 2)])
+            ext_c[...] = rows[pl.ds(0, 2), pl.ds(0, 2)]
+
+        @pl.when(jnp.logical_and(j == 4 + 2 * depth_of(1), v != 1))
         def _():
             corner_copy(ext_c, 0).wait_recv()
             corner_forward(ext_c)
 
-    @pl.loop(n, n + 2 * nbits)
+        compute(j)
+
+    @pl.loop(n, n + max(side_lag, row_lag))
     def _(j):
         for s in range(2):
             side_turn(s, j)
+        compute(j)
+
+    panels.finish_upper()
+    panels.finish()
 
     @pl.loop(0, n)
     def _(j):
@@ -231,12 +276,6 @@
                 down(k, j).wait_send()
 
             sib(k, j).wait_send()
-
-        sib_in(1, j).wait_recv()
-
-        @pl.when(j > 0)
-        def _():
-            sib_in(0, j).wait_recv()
 
         for s in range(2):
             for bi in range(nbits):
@@ -253,9 +292,6 @@
         ext_copy(ext_r.at[core], 1, other, 3).wait_send()
 
     ext_copy(ext_r.at[core], 2, other, 4).wait_send()
-    pltpu.make_async_remote_copy(
-        ext_r.at[core], ext_r.at[1 - core], e_sem.at[2], e_sem.at[4],
-        device_id={"prow": other, "pcol": v}, device_id_type=MESH).wait_recv()
     for bi in range(nbits):
         @pl.when(label(1) % (2 << bi) == 0)
         def _():
@@ -266,103 +302,117 @@
     return jnp.dot(a, b, preferred_element_type=jnp.float32)
 
 
-def update(
-    cols, place,
-    order, inverse, rows, side, ext_r, ext_c, tiles,
-    out,
-    m0, m1, r1, final,
-):
-    p = lax.axis_index("prow")
-    v = lax.axis_index("pcol")
-    bf = jnp.bfloat16
-    spread = lax.broadcasted_iota(jnp.int32, (256, 256), 1)
-    perm0 = (order[0] == spread).astype(bf)
-    perm1 = (order[1] == spread).astype(bf)
-    inv0, inv1 = inverse[0], inverse[1]
-    mix0 = dot(inv0, perm0).astype(bf)
-    mix1 = dot(inv1, perm1).astype(bf)
-    corner = jnp.concatenate(
-        [jnp.concatenate([ext_c[0, r], ext_c[1, r]], axis=1) for r in range(2)], axis=0)
-    pivot_rows = jnp.concatenate(
-        [jnp.concatenate([ext_r[r, 0], ext_r[r, 1]], axis=1) for r in range(2)], axis=0)
-    step = 4
-
-    @pl.loop(0, ROW_TILES, step=step)
-    def _(i):
+def pick(order, count):
+    spread = lax.broadcasted_iota(jnp.int32, (count, 256), 1)
+    return (order == spread).astype(jnp.bfloat16)
+
+
+class Panels:
+    def __init__(self, cols, order, inverse, rows, side, ext_r, ext_c, tiles, out, m0, m1, r1, final, place):
+        self.cols, self.order, self.inverse = cols, order, inverse
+        self.rows, self.side, self.ext_r, self.ext_c = rows, side, ext_r, ext_c
+        self.tiles, self.out, self.place = tiles, out, place
+        self.m0, self.m1, self.r1, self.final = m0, m1, r1, final
+        self.p = lax.axis_index("prow")
+        self.v = lax.axis_index("pcol")
+
+    def prepare(self, mixed):
+        for k in range(2):
+            mixed[k] = dot(self.inverse[k], pick(self.order[k], 256)).astype(jnp.bfloat16)
+        self.mixed = mixed
+
+    def side_step(self, i, step):
+        bf = jnp.bfloat16
+        ext_c, side, final, cols = self.ext_c, self.side, self.final, self.cols
+        corner = jnp.concatenate(
+            [jnp.concatenate([ext_c[0, r], ext_c[1, r]], axis=1) for r in range(2)], axis=0)
+
         def wide(s):
             return jnp.concatenate(
                 [side[s, pl.ds(i, step), h].reshape(step * 128, 128) for h in range(2)], axis=1)
 
         left = wide(0)
-        lower = dot(left, mix0).astype(bf)
-        m0[pl.ds(i, step)] = lower.reshape(step, 128, 256)
+        lower = dot(left, self.mixed[0]).astype(bf)
+        self.m0[pl.ds(i, step)] = lower.reshape(step, 128, 256)
         right = (wide(1).astype(jnp.float32) - dot(lower, corner)).astype(bf)
-        m1[pl.ds(i, step)] = dot(right, mix1).astype(bf).reshape(step, 128, 256)
+        self.m1[pl.ds(i, step)] = dot(right, self.mixed[1]).astype(bf).reshape(step, 128, 256)
 
         def keep(value):
             for u in range(step):
                 for h in range(2):
                     final[cols + 2 * (i + u) + h] = value[u * 128:(u + 1) * 128, h * 128:(h + 1) * 128]
 
-        @pl.when(v == 0)
-        def _():
-            keep(dot(left, inv0).astype(bf))
-
-        @pl.when(v == 1)
-        def _():
-            keep(dot(right, inv1).astype(bf))
-
-    lead = dot(pivot_rows, mix0).astype(bf)
-
-    @pl.loop(0, cols, step=step)
-    def _(c):
-        top = jnp.concatenate([rows[c + u, pl.ds(0, 2)].reshape(256, 128) for u in range(step)], axis=1)
-        low = jnp.concatenate([rows[c + u, pl.ds(2, 2)].reshape(256, 128) for u in range(step)], axis=1)
-        value = (low.astype(jnp.float32) - dot(lead, top)).astype(bf)
+        @pl.when(self.v == 0)
+        def _():
+            keep(dot(left, self.inverse[0]).astype(bf))
+
+        @pl.when(self.v == 1)
+        def _():
+            keep(dot(right, self.inverse[1]).astype(bf))
+
+    def pivot_rows(self):
+        ext_r = self.ext_r
+        return jnp.concatenate(
+            [jnp.concatenate([ext_r[r, 0], ext_r[r, 1]], axis=1) for r in range(2)], axis=0)
+
+    def set_lead(self):
+        self.lead[...] = dot(self.pivot_rows(), self.mixed[0]).astype(jnp.bfloat16)
+
+    def stacked(self, c, step, half):
+        return jnp.concatenate(
+            [self.rows[c + u, pl.ds(2 * half, 2)].reshape(256, 128) for u in range(step)], axis=1)
+
+    def row_step(self, c, step):
+        top = self.stacked(c, step, 0)
+        low = self.stacked(c, step, 1)
+        value = (low.astype(jnp.float32) - dot(self.lead[...], top)).astype(jnp.bfloat16)
         for u in range(step):
-            r1[c + u] = value[:, u * 128:(u + 1) * 128]
-
-    @pl.when(v == 0)
-    def _():
-        value = dot(pivot_rows, inv0).astype(bf)
-        r1[0] = value[:, :128]
-        r1[1] = value[:, 128:]
-
-    narrow = lax.broadcasted_iota(jnp.int32, (128, 256), 1)
-
-    @pl.when(p < 2)
-    def _():
-        part = (order[0, pl.ds(p * 128, 128)] == narrow).astype(bf)
-
-        @pl.loop(0, cols, step=step)
-        def _(c):
-            top = jnp.concatenate([rows[c + u, pl.ds(0, 2)].reshape(256, 128) for u in range(step)], axis=1)
-            value = dot(part, top).astype(bf)
-            for u in range(step):
-                final[c + u] = value[:, u * 128:(u + 1) * 128]
-
-    @pl.when(jnp.logical_and(p >= 2, p < 4))
-    def _():
-        part = (order[1, pl.ds((p - 2) * 128, 128)] == narrow).astype(bf)
-
-        @pl.loop(0, cols, step=step)
-        def _(c):
-            low = jnp.concatenate([r1[c + u] for u in range(step)], axis=1)
-            value = dot(part, low).astype(bf)
-            for u in range(step):
-                final[c + u] = value[:, u * 128:(u + 1) * 128]
-
-    slots = tiles.shape[0]
-
-    @pl.loop(0, slots, step=GROUP)
-    def _(base):
-        for u in range(GROUP):
-            s = base + u
-            i, c, f, kind = place[0, s], place[1, s], place[2, s], place[3, s]
-            old = tiles[s].astype(jnp.float32)
-            total = dot(m0[i], rows[c, pl.ds(0, 2)].reshape(256, 128)) + dot(m1[i], r1[c])
-            other = jnp.where(kind == 1, final[f].astype(jnp.float32), old)
-            out[s] = jnp.where(kind == 0, old - total, other).astype(bf)
+            self.r1[c + u] = value[:, u * 128:(u + 1) * 128]
+
+    def finish_upper(self):
+        bf = jnp.bfloat16
+        p, r1, final, cols = self.p, self.r1, self.final, self.cols
+        step = 4
+
+        @pl.when(self.v == 0)
+        def _():
+            value = dot(self.pivot_rows(), self.inverse[0]).astype(bf)
+            r1[0] = value[:, :128]
+            r1[1] = value[:, 128:]
+
+        @pl.when(p < 2)
+        def _():
+            part = pick(self.order[0, pl.ds(p * 128, 128)], 128)
+
+            @pl.loop(0, cols, step=step)
+            def _(c):
+                value = dot(part, self.stacked(c, step, 0)).astype(bf)
+                for u in range(step):
+                    final[c + u] = value[:, u * 128:(u + 1) * 128]
+
+        @pl.when(jnp.logical_and(p >= 2, p < 4))
+        def _():
+            part = pick(self.order[1, pl.ds((p - 2) * 128, 128)], 128)
+
+            @pl.loop(0, cols, step=step)
+            def _(c):
+                low = jnp.concatenate([r1[c + u] for u in range(step)], axis=1)
+                value = dot(part, low).astype(bf)
+                for u in range(step):
+                    final[c + u] = value[:, u * 128:(u + 1) * 128]
+
+    def finish(self):
+        place, tiles, rows, final = self.place, self.tiles, self.rows, self.final
+
+        @pl.loop(0, tiles.shape[0], step=GROUP)
+        def _(base):
+            for u in range(GROUP):
+                s = base + u
+                i, c, f, kind = place[0, s], place[1, s], place[2, s], place[3, s]
+                old = tiles[s].astype(jnp.float32)
+                total = dot(self.m0[i], rows[c, pl.ds(0, 2)].reshape(256, 128)) + dot(self.m1[i], self.r1[c])
+                other = jnp.where(kind == 1, final[f].astype(jnp.float32), old)
+                self.out[s] = jnp.where(kind == 0, old - total, other).astype(jnp.bfloat16)
 
 
 def local(tiles, tile_pos, pivots, inverses):
@@ -392,38 +442,30 @@
     vmem = pl.BlockSpec(memory_space=pltpu.VMEM)
     dma = pltpu.SemaphoreType.DMA
     n = CHUNKS
-    rows, side, ext_r, ext_c = pl.pallas_call(
+    panel = 2 * edge
+    return pl.pallas_call(
         functools.partial(exchange, nz, nbits, cols),
-        out_shape=[
-            jax.ShapeDtypeStruct((cols, 4, edge, edge), bf),
-            jax.ShapeDtypeStruct((2, ROW_TILES, 2, edge, edge), bf),
-            jax.ShapeDtypeStruct((2, 2, edge, edge), bf),
-            jax.ShapeDtypeStruct((2, 2, edge, edge), bf),
-        ],
-        in_specs=[smem, smem, vmem],
-        out_specs=[vmem] * 4,
+        out_shape=jax.ShapeDtypeStruct(tiles.shape, bf),
+        in_specs=[smem, smem, smem, vmem, vmem, vmem],
+        out_specs=vmem,
         scratch_shapes=[
+            pltpu.VMEM((cols, 4, edge, edge), bf),
+            pltpu.VMEM((2, ROW_TILES, 2, edge, edge), bf),
+            pltpu.VMEM((2, 2, edge, edge), bf),
+            pltpu.VMEM((2, 2, edge, edge), bf),
+            pltpu.VMEM((ROW_TILES, edge, panel), bf),
+            pltpu.VMEM((ROW_TILES, edge, panel), bf),
+            pltpu.VMEM((cols, panel, edge), bf),
+            pltpu.VMEM((cols + 2 * ROW_TILES, edge, edge), bf),
+            pltpu.VMEM((2, panel, panel), bf),
+            pltpu.VMEM((panel, panel), bf),
             dma((2, n)), dma((2, n)), dma((2, n)), dma((2, n)), dma((2, n)),
             dma((2, nbits, n)), dma((2, n)), dma((5,)), dma((nbits,)), dma((1,)),
         ],
         compiler_params=pltpu.CompilerParams(
-            collective_id=0, has_side_effects=True, vmem_limit_bytes=40 * 1024 * 1024),
+            collective_id=0, has_side_effects=True, vmem_limit_bytes=48 * 1024 * 1024),
         name="exchange",
-    )(slot_r, slot_l, tiles)
-    return pl.pallas_call(
-        functools.partial(update, cols),
-        out_shape=jax.ShapeDtypeStruct(tiles.shape, bf),
-        in_specs=[smem] + [vmem] * 7,
-        out_specs=vmem,
-        scratch_shapes=[
-            pltpu.VMEM((ROW_TILES, edge, 2 * edge), bf),
-            pltpu.VMEM((ROW_TILES, edge, 2 * edge), bf),
-            pltpu.VMEM((cols, 2 * edge, edge), bf),
-            pltpu.VMEM((cols + 2 * ROW_TILES, edge, edge), bf),
-        ],
-        compiler_params=pltpu.CompilerParams(vmem_limit_bytes=48 * 1024 * 1024),
-        name="update",
-    )(place, pivots.reshape(2, 2 * edge, 1), inverses, rows, side, ext_r, ext_c, tiles)
+    )(slot_r, slot_l, place, pivots.reshape(2, panel, 1), inverses, tiles)
 
 
 def solution(mesh):

time: 145 us -> 131 us (0.903)
  Pallas kernels: 140 us -> 125 us
    pallas_call x2 -> x1, Pallas kernels: 140 us -> 125 us  [local(): pl.pallas_call(functools.partial(exchange, nz, nbits, cols), out_shape=ja...]
    unnamed x4 -> x3, local copies, waits for them, and re-layouts: 2.19 us -> 2.96 us
where the time goes in v3:
time: 131 us
  Pallas kernels  125 us (95%)
  local copies, waits for them, and re-layouts  3.79 us (3%)
  other arithmetic  1.68 us (1%)
    pallas_call x1, Pallas kernels, local(): pl.pallas_call(functools.partial(exchange, nz, nbits, cols), out_shape=ja...  125 us
    unnamed x3, local copies, waits for them, and re-layouts  2.96 us

profile of v3, /device:TPU:28, one launch (start us, length us, event | category | flops | bytes accessed | tf_op | source)
XLA Modules:
  0.0 130.8 jit_solution(16515032209299714127)
XLA Ops:
  0.0 0.8 and_select_fusion.5
  0.8 0.1 select_reduce_fusion
  0.9 0.8 compare_select_fusion
  1.7 0.8 copy.6.order
  2.5 0.0 copy-start
  2.5 0.9 copy-done
  3.5 125.3 %exchange.1 = bf16[128,128,128]{2,1,0:T(8,128)(2,1)S(1)} custom-call(s32[64]{0:T(128)S(1)} %get-tuple-element.12.slot_r, s32[64]{0:T(128)S(1)} %get-tuple-element.11.slot_l, s32[4,128]{1,0:T(4,128)S(1)} %pad_add_fusion.place, s32[2,256,1]{2,1,0:T(8,128)S(1)} %copy.6.order, bf16[2,256,256]{2,1,0:T(8,128)(2,1)S(1)} %copy-done, bf16[128,128,128]{2,1,0:T(8,128)(2,1)} %tiles.1), custom_call_target="tpu_custom_call" | custom-call | tf_op jit(solution)/shard_map/exchange/pallas_call | solution.py:446
  128.8 2.0 %copy.8 = bf16[128,128,128]{2,1,0:T(8,128)(2,1)} copy(bf16[128,128,128]{2,1,0:T(8,128)(2,1)S(1)} %exchange.1) | data formatting | bytes 8388608
  (1 shorter events, 0.0 us)
Async XLA Ops:
  2.5 1.0 copy-start

commit v4 on v3

v4 whole, which is shorter than its diff:
```python
import functools
import jax
import jax.numpy as jnp
from jax import lax
from jax.experimental import pallas as pl
from jax.experimental.pallas import tpu as pltpu
from jax.sharding import PartitionSpec as P

ROW_TILES = 32
CHUNKS = 32
AHEAD = 3
GROUP = 16
SIDE_CHUNKS = 16
MESH = pl.DeviceIdType.MESH


def slot_lookup(keys, count):
    targets = jnp.arange(count, dtype=jnp.int32)
    matches = keys[None, :] == targets[:, None]
    positions = jnp.arange(keys.shape[0], dtype=jnp.int32)
    return jnp.sum(jnp.where(matches, positions[None, :], 0), axis=1)


def exchange(
    nz, nbits, cols,
    slot_r, slot_l, place, order, inverse, tiles,
    out,
    rows, side, ext_r, ext_c, mix, both, final, mixed, lead,
    up_send, down_send, sib_send, z_recv, sib_recv,
    l_send, l_recv, e_sem, f_send, f_recv,
):
    p = lax.axis_index("prow")
    v = lax.axis_index("pcol")
    z = p // 2
    core = p % 2
    other = p + 1 - 2 * core
    cw = cols // CHUNKS
    ns = SIDE_CHUNKS
    rw = ROW_TILES // ns
    n = CHUNKS
    step = 4
    per = step // cw
    row_lag = 4 * ((3 * nbits + 2 * nz + 1) // 4)
    catch_up = per * (row_lag - 1) // (per - 1)
    panels = Panels(cols, order, inverse, rows, side, ext_r, ext_c, tiles, out, mix, both, final, place)
    panels.lead = lead

    def flip(b):
        return v + b - 2 * b * ((v // b) % 2)

    barrier = pltpu.get_barrier_semaphore()

    @pl.when(z > 0)
    def _():
        pl.semaphore_signal(barrier, inc=1, device_id={"prow": p - 2, "pcol": v}, device_id_type=MESH)

    @pl.when(z < nz - 1)
    def _():
        pl.semaphore_signal(barrier, inc=1, device_id={"prow": p + 2, "pcol": v}, device_id_type=MESH)

    pl.semaphore_signal(barrier, inc=1, device_id={"prow": other, "pcol": v}, device_id_type=MESH)
    for bi in range(nbits):
        pl.semaphore_signal(barrier, inc=1, device_id={"prow": p, "pcol": flip(1 << bi)}, device_id_type=MESH)

    @pl.when(z < 2)
    def _():
        @pl.loop(0, cols)
        def _(c):
            rows[c, p] = tiles[slot_r[c]]

    ends = (z == 0).astype(jnp.int32) + (z == nz - 1).astype(jnp.int32)
    pl.semaphore_wait(barrier, 3 + nbits - ends)

    def block(k, j):
        return rows.at[pl.ds(j * cw, cw), 2 * k + core]

    def up(k, j):
        return pltpu.make_async_remote_copy(
            block(k, j), block(k, j), up_send.at[k, j], z_recv.at[k, j],
            device_id={"prow": p + 2, "pcol": v}, device_id_type=MESH)

    def down(k, j):
        return pltpu.make_async_remote_copy(
            block(k, j), block(k, j), down_send.at[k, j], z_recv.at[k, j],
            device_id={"prow": p - 2, "pcol": v}, device_id_type=MESH)

    def sib(k, j):
        return pltpu.make_async_remote_copy(
            block(k, j), block(k, j), sib_send.at[k, j], sib_recv.at[k, j],
            device_id={"prow": other, "pcol": v}, device_id_type=MESH)

    def sib_in(k, j):
        there = rows.at[pl.ds(j * cw, cw), 2 * k + 1 - core]
        return pltpu.make_async_remote_copy(
            there, there, sib_send.at[k, j], sib_recv.at[k, j],
            device_id={"prow": other, "pcol": v}, device_id_type=MESH)

    def goes_up(k):
        return jnp.logical_and(z >= k, z < nz - 1)

    def goes_down(k):
        return jnp.logical_and(z <= k, z > 0)

    def forward(k, j):
        @pl.when(goes_up(k))
        def _():
            up(k, j).start()

        @pl.when(goes_down(k))
        def _():
            down(k, j).start()

        sib(k, j).start()

    def own(k, j):
        @pl.when(z == k)
        def _():
            forward(k, j)

    def label(s):
        return v if s == 0 else v + 1 - 2 * (v % 2)

    def side_copy(s, j, bi):
        part = side.at[s, pl.ds(j * rw, rw)]
        return pltpu.make_async_remote_copy(
            part, part, l_send.at[s, bi, j], l_recv.at[s, j],
            device_id={"prow": p, "pcol": flip(1 << bi)}, device_id_type=MESH)

    def side_forward(s, j):
        for bi in range(nbits):
            @pl.when(label(s) % (2 << bi) == 0)
            def _():
                side_copy(s, j, bi).start()

    def ext_copy(source, sem, target, recv):
        return pltpu.make_async_remote_copy(
            source, ext_r.at[core], e_sem.at[sem], e_sem.at[recv],
            device_id={"prow": target, "pcol": v}, device_id_type=MESH)

    def ext_forward(source):
        @pl.when(goes_up(1))
        def _():
            ext_copy(source, 0, p + 2, 3).start()

        @pl.when(goes_down(1))
        def _():
            ext_copy(source, 1, p - 2, 3).start()

        ext_copy(source, 2, other, 4).start()

    def corner_copy(source, bi):
        return pltpu.make_async_remote_copy(
            source, ext_c, f_send.at[bi], f_recv.at[0],
            device_id={"prow": p, "pcol": flip(1 << bi)}, device_id_type=MESH)

    def corner_forward(source):
        for bi in range(nbits):
            @pl.when(label(1) % (2 << bi) == 0)
            def _():
                corner_copy(source, bi).start()

    def depth_of(s):
        return sum((label(s) // (1 << bi)) % 2 for bi in range(nbits))

    def side_turns(j):
        @pl.when(j % 4 != 3)
        def _():
            for s in range(2):
                side_turn(s, 3 * (j // 4) + j % 4)

    def compute(j):
        at = 3 * (j // 4) + j % 4 - 2 * nbits - 2

        @pl.when(jnp.logical_and(j % 4 != 3, jnp.logical_and(at >= 0, at < ns)))
        def _():
            @pl.when(at % (step // rw) == 0)
            def _():
                panels.side_step(at * rw, step)

        @pl.when(j == row_lag)
        def _():
            pltpu.make_async_remote_copy(
                ext_r.at[core], ext_r.at[1 - core], e_sem.at[2], e_sem.at[4],
                device_id={"prow": other, "pcol": v}, device_id_type=MESH).wait_recv()
            panels.set_lead()

        early = jnp.logical_and(j >= row_lag, j <= catch_up)
        late = jnp.logical_and(j > catch_up, j % per == 0)
        first = per * jnp.where(j <= catch_up, j - row_lag, j // per - 1)

        @pl.when(jnp.logical_and(jnp.logical_or(early, late), first < n))
        def _():
            for h in range(per):
                sib_in(1, first + h).wait_recv()

                @pl.when(jnp.logical_or(v != 1, (first + h) * cw >= 2))
                def _():
                    sib_in(0, first + h).wait_recv()

            panels.row_step(first * cw, step)

    def side_turn(s, j):
        depth = depth_of(s)
        at = j - 2 * depth + jnp.where(depth > 0, 1, 0)

        @pl.when(jnp.logical_and(at >= 0, at < ns))
        def _():
            @pl.when(depth > 0)
            def _():
                side_copy(s, at, 0).wait_recv()

            side_forward(s, at)

    for k in range(2):
        for j in range(AHEAD):
            own(k, j)

    @pl.when(v < 2)
    def _():
        @pl.loop(0, ROW_TILES)
        def _(i):
            side[v, i, 0] = tiles[slot_l[2 * i]]
            side[v, i, 1] = tiles[slot_l[2 * i + 1]]

    panels.prepare(mixed)

    @pl.loop(0, n)
    def _(j):
        @pl.when(j + AHEAD < n)
        def _():
            own(0, j + AHEAD)
            own(1, j + AHEAD)

        for k in (1, 0):
            @pl.when(z != k)
            def _():
                up(k, j).wait_recv()
                forward(k, j)

        side_turns(j)

        @pl.when(jnp.logical_and(j == 3 * nbits, z == 1))
        def _():
            ext_forward(side.at[0, 0])
            ext_r[core] = side[0, 0]

        far = jnp.where(z == 0, 1, z - 1)

        @pl.when(jnp.logical_and(j == 3 * nbits + 2 * far, z != 1))
        def _():
            ext_copy(ext_r.at[core], 0, other, 3).wait_recv()
            ext_forward(ext_r.at[core])

        @pl.when(jnp.logical_and(j == 4, v == 1))
        def _():
            for h in range(2 // min(cw, 2)):
                sib_in(0, h).wait_recv()
            corner_forward(rows.at[pl.ds(0, 2), pl.ds(0, 2)])
            ext_c[...] = rows[pl.ds(0, 2), pl.ds(0, 2)]

        @pl.when(jnp.logical_and(j == 4 + 2 * depth_of(1), v != 1))
        def _():
            corner_copy(ext_c, 0).wait_recv()
            corner_forward(ext_c)

        compute(j)

    @pl.loop(n, n + 8)
    def _(j):
        side_turns(j)
        compute(j)

    panels.finish_upper()
    panels.finish()

    @pl.loop(0, n)
    def _(j):
        for k in range(2):
            @pl.when(goes_up(k))
            def _():
                up(k, j).wait_send()

            @pl.when(goes_down(k))
            def _():
                down(k, j).wait_send()

            sib(k, j).wait_send()

    @pl.loop(0, ns)
    def _(j):
        for s in range(2):
            for bi in range(nbits):
                @pl.when(label(s) % (2 << bi) == 0)
                def _():
                    side_copy(s, j, bi).wait_send()

    @pl.when(goes_up(1))
    def _():
        ext_copy(ext_r.at[core], 0, other, 3).wait_send()

    @pl.when(goes_down(1))
    def _():
        ext_copy(ext_r.at[core], 1, other, 3).wait_send()

    ext_copy(ext_r.at[core], 2, other, 4).wait_send()
    for bi in range(nbits):
        @pl.when(label(1) % (2 << bi) == 0)
        def _():
            corner_copy(ext_c, bi).wait_send()


def dot(a, b):
    return jnp.dot(a, b, preferred_element_type=jnp.float32)


def pick(order, count):
    spread = lax.broadcasted_iota(jnp.int32, (count, 256), 1)
    return (order == spread).astype(jnp.bfloat16)


class Panels:
    def __init__(self, cols, order, inverse, rows, side, ext_r, ext_c, tiles, out, mix, both, final, place):
        self.cols, self.order, self.inverse = cols, order, inverse
        self.rows, self.side, self.ext_r, self.ext_c = rows, side, ext_r, ext_c
        self.tiles, self.out, self.place = tiles, out, place
        self.mix, self.both, self.final = mix, both, final
        self.p = lax.axis_index("prow")
        self.v = lax.axis_index("pcol")

    def prepare(self, mixed):
        for k in range(2):
            mixed[k] = dot(self.inverse[k], pick(self.order[k], 256)).astype(jnp.bfloat16)
        self.mixed = mixed

    def side_step(self, i, step):
        bf = jnp.bfloat16
        ext_c, side, final, cols = self.ext_c, self.side, self.final, self.cols
        corner = jnp.concatenate(
            [jnp.concatenate([ext_c[0, r], ext_c[1, r]], axis=1) for r in range(2)], axis=0)

        def wide(s):
            return jnp.concatenate(
                [side[s, pl.ds(i, step), h].reshape(step * 128, 128) for h in range(2)], axis=1)

        left = wide(0)
        lower = dot(left, self.mixed[0]).astype(bf)
        self.mix[pl.ds(i, step), :, pl.ds(0, 256)] = lower.reshape(step, 128, 256)
        right = (wide(1).astype(jnp.float32) - dot(lower, corner)).astype(bf)
        self.mix[pl.ds(i, step), :, pl.ds(256, 256)] = dot(right, self.mixed[1]).astype(bf).reshape(step, 128, 256)

        def keep(value):
            for u in range(step):
                for h in range(2):
                    final[cols + 2 * (i + u) + h] = value[u * 128:(u + 1) * 128, h * 128:(h + 1) * 128]

        @pl.when(self.v == 0)
        def _():
            keep(dot(left, self.inverse[0]).astype(bf))

        @pl.when(self.v == 1)
        def _():
            keep(dot(right, self.inverse[1]).astype(bf))

    def pivot_rows(self):
        ext_r = self.ext_r
        return jnp.concatenate(
            [jnp.concatenate([ext_r[r, 0], ext_r[r, 1]], axis=1) for r in range(2)], axis=0)

    def set_lead(self):
        self.lead[...] = dot(self.pivot_rows(), self.mixed[0]).astype(jnp.bfloat16)

    def stacked(self, c, step, half):
        return jnp.concatenate(
            [self.rows[c + u, pl.ds(2 * half, 2)].reshape(256, 128) for u in range(step)], axis=1)

    def row_step(self, c, step):
        top = self.stacked(c, step, 0)
        low = self.stacked(c, step, 1)
        value = (low.astype(jnp.float32) - dot(self.lead[...], top)).astype(jnp.bfloat16)
        for u in range(step):
            self.both[c + u, pl.ds(0, 256)] = top[:, u * 128:(u + 1) * 128]
            self.both[c + u, pl.ds(256, 256)] = value[:, u * 128:(u + 1) * 128]

    def finish_upper(self):
        bf = jnp.bfloat16
        p, both, final, cols = self.p, self.both, self.final, self.cols
        step = 4

        @pl.when(self.v == 0)
        def _():
            value = dot(self.pivot_rows(), self.inverse[0]).astype(bf)
            both[0, pl.ds(256, 256)] = value[:, :128]
            both[1, pl.ds(256, 256)] = value[:, 128:]

        @pl.when(p < 2)
        def _():
            part = pick(self.order[0, pl.ds(p * 128, 128)], 128)

            @pl.loop(0, cols, step=step)
            def _(c):
                value = dot(part, self.stacked(c, step, 0)).astype(bf)
                for u in range(step):
                    final[c + u] = value[:, u * 128:(u + 1) * 128]

        @pl.when(jnp.logical_and(p >= 2, p < 4))
        def _():
            part = pick(self.order[1, pl.ds((p - 2) * 128, 128)], 128)

            @pl.loop(0, cols, step=step)
            def _(c):
                low = jnp.concatenate([both[c + u, pl.ds(256, 256)] for u in range(step)], axis=1)
                value = dot(part, low).astype(bf)
                for u in range(step):
                    final[c + u] = value[:, u * 128:(u + 1) * 128]

    def finish(self):
        place, tiles, final = self.place, self.tiles, self.final

        @pl.loop(0, tiles.shape[0], step=GROUP)
        def _(base):
            for u in range(GROUP):
                s = base + u
                i, c, f, kind = place[0, s], place[1, s], place[2, s], place[3, s]
                base_value = jnp.where(kind == 1, final[f], tiles[s]).astype(jnp.float32)
                total = dot(self.mix[i], self.both[c])
                self.out[s] = (base_value - jnp.where(kind == 0, 1.0, 0.0) * total).astype(jnp.bfloat16)


def local(tiles, tile_pos, pivots, inverses):
    slots, edge, _ = tiles.shape
    row_procs = lax.axis_size("prow")
    col_procs = lax.axis_size("pcol")
    nz = row_procs // 2
    nbits = col_procs.bit_length() - 1
    cols = ROW_TILES * row_procs // col_procs
    tile_row = tile_pos[:, 0]
    tile_col = tile_pos[:, 1]
    local_row = jnp.clip(tile_row // row_procs, 0, ROW_TILES - 1)
    local_col = jnp.clip(2 * (tile_col // 2 // col_procs) + tile_col % 2, 0, cols - 1)
    listed = tile_row >= 0
    is_upper = listed & (tile_row < 4)
    is_side = listed & (tile_col < 4)
    side_key = local_row * 2 + tile_col % 2
    slot_r = slot_lookup(jnp.where(is_upper, local_col, -1), cols)
    slot_l = slot_lookup(jnp.where(is_side, side_key, -1), 2 * ROW_TILES)
    done = jnp.where(is_upper, local_col, cols + side_key)
    kind = jnp.where(listed, jnp.where(is_upper | is_side, 1, 0), 2)
    done = jnp.where(kind == 1, done, 0)
    place = jnp.stack([local_row, local_col, done, kind]).astype(jnp.int32)

    bf = jnp.bfloat16
    smem = pl.BlockSpec(memory_space=pltpu.SMEM)
    vmem = pl.BlockSpec(memory_space=pltpu.VMEM)
    dma = pltpu.SemaphoreType.DMA
    n = CHUNKS
    panel = 2 * edge
    return pl.pallas_call(
        functools.partial(exchange, nz, nbits, cols),
        out_shape=jax.ShapeDtypeStruct(tiles.shape, bf),
        in_specs=[smem, smem, smem, vmem, vmem, vmem],
        out_specs=vmem,
        scratch_shapes=[
            pltpu.VMEM((cols, 4, edge, edge), bf),
            pltpu.VMEM((2, ROW_TILES, 2, edge, edge), bf),
            pltpu.VMEM((2, 2, edge, edge), bf),
            pltpu.VMEM((2, 2, edge, edge), bf),
            pltpu.VMEM((ROW_TILES, edge, 2 * panel), bf),
            pltpu.VMEM((cols, 2 * panel, edge), bf),
            pltpu.VMEM((cols + 2 * ROW_TILES, edge, edge), bf),
            pltpu.VMEM((2, panel, panel), bf),
            pltpu.VMEM((panel, panel), bf),
            dma((2, n)), dma((2, n)), dma((2, n)), dma((2, n)), dma((2, n)),
            dma((2, nbits, SIDE_CHUNKS)), dma((2, SIDE_CHUNKS)), dma((5,)), dma((nbits,)), dma((1,)),
        ],
        compiler_params=pltpu.CompilerParams(
            collective_id=0, has_side_effects=True, vmem_limit_bytes=48 * 1024 * 1024),
        name="exchange",
    )(slot_r, slot_l, place, pivots.reshape(2, panel, 1), inverses, tiles)


def solution(mesh):
    return jax.shard_map(
        local,
        mesh=mesh,
        in_specs=(P(("prow", "pcol"), None, None), P(("prow", "pcol"), None), P(), P()),
        out_specs=P(("prow", "pcol"), None, None),
        check_vma=False,
    )
```

time: 131 us -> 124 us (0.947); the launches traced: 131 us -> 121 us
  Pallas kernels: 125 us -> 116 us
    pallas_call x1, Pallas kernels: 125 us -> 116 us  [local(): pl.pallas_call(functools.partial(exchange, nz, nbits, cols), out_shape=ja...]
where the time goes in v4:
time: 124 us; the launch traced here: 121 us
  Pallas kernels  116 us (94%)
  local copies, waits for them, and re-layouts  3.79 us (3%)
  other arithmetic  1.68 us (1%)
    pallas_call x1, Pallas kernels, local(): pl.pallas_call(functools.partial(exchange, nz, nbits, cols), out_shape=ja...  116 us
    unnamed x3, local copies, waits for them, and re-layouts  2.96 us

profile of v4, /device:TPU:28, one launch (start us, length us, event | category | flops | bytes accessed | tf_op | source)
XLA Modules:
  0.0 121.5 jit_solution(15400053108514452236)
XLA Ops:
  0.0 0.8 and_select_fusion.5
  0.8 0.1 select_reduce_fusion
  0.9 0.8 compare_select_fusion
  1.7 0.8 copy.6.order
  2.5 0.0 copy-start
  2.5 0.9 copy-done
  3.5 116.0 %exchange.1 = bf16[128,128,128]{2,1,0:T(8,128)(2,1)S(1)} custom-call(s32[64]{0:T(128)S(1)} %get-tuple-element.12.slot_r, s32[64]{0:T(128)S(1)} %get-tuple-element.11.slot_l, s32[4,128]{1,0:T(4,128)S(1)} %pad_add_fusion.place, s32[2,256,1]{2,1,0:T(8,128)S(1)} %copy.6.order, bf16[2,256,256]{2,1,0:T(8,128)(2,1)S(1)} %copy-done, bf16[128,128,128]{2,1,0:T(8,128)(2,1)} %tiles.1), custom_call_target="tpu_custom_call" | custom-call | tf_op jit(solution)/shard_map/exchange/pallas_call | solution.py:457
  119.4 2.0 %copy.8 = bf16[128,128,128]{2,1,0:T(8,128)(2,1)} copy(bf16[128,128,128]{2,1,0:T(8,128)(2,1)S(1)} %exchange.1) | data formatting | bytes 8388608
  (1 shorter events, 0.0 us)
Async XLA Ops:
  2.5 1.0 copy-start

commit v5 on v4

--- a/solution.py
+++ b/solution.py
@@ -7,40 +7,33 @@
 from jax.sharding import PartitionSpec as P
 
 ROW_TILES = 32
-CHUNKS = 32
 AHEAD = 3
 GROUP = 16
 SIDE_CHUNKS = 16
 MESH = pl.DeviceIdType.MESH
 
 
-def slot_lookup(keys, count):
-    targets = jnp.arange(count, dtype=jnp.int32)
-    matches = keys[None, :] == targets[:, None]
-    positions = jnp.arange(keys.shape[0], dtype=jnp.int32)
-    return jnp.sum(jnp.where(matches, positions[None, :], 0), axis=1)
-
-
 def exchange(
     nz, nbits, cols,
-    slot_r, slot_l, place, order, inverse, tiles,
+    slots, place, order, inverse_in, tiles_in,
     out,
-    rows, side, ext_r, ext_c, mix, both, final, mixed, lead,
+    tiles, inverse, perm, rows, side, ext_r, ext_c, mix, both, final, mixed, lead,
     up_send, down_send, sib_send, z_recv, sib_recv,
-    l_send, l_recv, e_sem, f_send, f_recv,
+    l_send, l_recv, e_sem, f_send, f_recv, in_sem,
 ):
     p = lax.axis_index("prow")
     v = lax.axis_index("pcol")
     z = p // 2
     core = p % 2
     other = p + 1 - 2 * core
-    cw = cols // CHUNKS
+    n = cols
+    cw = 1
+    stretch = max(n // 32, 1)
     ns = SIDE_CHUNKS
     rw = ROW_TILES // ns
-    n = CHUNKS
     step = 4
     per = step // cw
-    row_lag = 4 * ((3 * nbits + 2 * nz + 1) // 4)
+    row_lag = 4 * stretch * ((3 * nbits + 2 * nz + 1) // 4)
     catch_up = per * (row_lag - 1) // (per - 1)
     panels = Panels(cols, order, inverse, rows, side, ext_r, ext_c, tiles, out, mix, both, final, place)
     panels.lead = lead
@@ -48,6 +41,10 @@
     def flip(b):
         return v + b - 2 * b * ((v // b) % 2)
 
+    load_tiles = pltpu.make_async_copy(tiles_in, tiles, in_sem.at[0])
+    load_inverse = pltpu.make_async_copy(inverse_in, inverse, in_sem.at[1])
+    load_tiles.start()
+    load_inverse.start()
     barrier = pltpu.get_barrier_semaphore()
 
     @pl.when(z > 0)
@@ -62,11 +59,13 @@
     for bi in range(nbits):
         pl.semaphore_signal(barrier, inc=1, device_id={"prow": p, "pcol": flip(1 << bi)}, device_id_type=MESH)
 
+    load_tiles.wait()
+
     @pl.when(z < 2)
     def _():
         @pl.loop(0, cols)
         def _(c):
-            rows[c, p] = tiles[slot_r[c]]
+            rows[c, p] = tiles[slots[c]]
 
     ends = (z == 0).astype(jnp.int32) + (z == nz - 1).astype(jnp.int32)
     pl.semaphore_wait(barrier, 3 + nbits - ends)
@@ -163,15 +162,19 @@
         return sum((label(s) // (1 << bi)) % 2 for bi in range(nbits))
 
     def side_turns(j):
-        @pl.when(j % 4 != 3)
+        slow = j // stretch
+
+        @pl.when(jnp.logical_and(j % stretch == 0, slow % 4 != 3))
         def _():
             for s in range(2):
-                side_turn(s, 3 * (j // 4) + j % 4)
+                side_turn(s, 3 * (slow // 4) + slow % 4)
 
     def compute(j):
-        at = 3 * (j // 4) + j % 4 - 2 * nbits - 2
-
-        @pl.when(jnp.logical_and(j % 4 != 3, jnp.logical_and(at >= 0, at < ns)))
+        slow = j // stretch
+        at = 3 * (slow // 4) + slow % 4 - 2 * nbits - 2
+        live = jnp.logical_and(j % stretch == stretch - 1, slow % 4 != 3)
+
+        @pl.when(jnp.logical_and(live, jnp.logical_and(at >= 0, at < ns)))
         def _():
             @pl.when(at % (step // rw) == 0)
             def _():
@@ -219,10 +222,11 @@
     def _():
         @pl.loop(0, ROW_TILES)
         def _(i):
-            side[v, i, 0] = tiles[slot_l[2 * i]]
-            side[v, i, 1] = tiles[slot_l[2 * i + 1]]
-
-    panels.prepare(mixed)
+            side[v, i, 0] = tiles[slots[cols + 2 * i]]
+            side[v, i, 1] = tiles[slots[cols + 2 * i + 1]]
+
+    load_inverse.wait()
+    panels.prepare(mixed, perm)
 
     @pl.loop(0, n)
     def _(j):
@@ -239,33 +243,33 @@
 
         side_turns(j)
 
-        @pl.when(jnp.logical_and(j == 3 * nbits, z == 1))
+        @pl.when(jnp.logical_and(j == stretch * 3 * nbits, z == 1))
         def _():
             ext_forward(side.at[0, 0])
             ext_r[core] = side[0, 0]
 
         far = jnp.where(z == 0, 1, z - 1)
 
-        @pl.when(jnp.logical_and(j == 3 * nbits + 2 * far, z != 1))
+        @pl.when(jnp.logical_and(j == stretch * (3 * nbits + 2 * far), z != 1))
         def _():
             ext_copy(ext_r.at[core], 0, other, 3).wait_recv()
             ext_forward(ext_r.at[core])
 
-        @pl.when(jnp.logical_and(j == 4, v == 1))
+        @pl.when(jnp.logical_and(j == stretch * 4, v == 1))
         def _():
             for h in range(2 // min(cw, 2)):
                 sib_in(0, h).wait_recv()
             corner_forward(rows.at[pl.ds(0, 2), pl.ds(0, 2)])
             ext_c[...] = rows[pl.ds(0, 2), pl.ds(0, 2)]
 
-        @pl.when(jnp.logical_and(j == 4 + 2 * depth_of(1), v != 1))
+        @pl.when(jnp.logical_and(j == stretch * (4 + 2 * depth_of(1)), v != 1))
         def _():
             corner_copy(ext_c, 0).wait_recv()
             corner_forward(ext_c)
 
         compute(j)
 
-    @pl.loop(n, n + 8)
+    @pl.loop(n, n + 8 * stretch)
     def _(j):
         side_turns(j)
         compute(j)
@@ -311,11 +315,6 @@
 
 def dot(a, b):
     return jnp.dot(a, b, preferred_element_type=jnp.float32)
-
-
-def pick(order, count):
-    spread = lax.broadcasted_iota(jnp.int32, (count, 256), 1)
-    return (order == spread).astype(jnp.bfloat16)
 
 
 class Panels:
@@ -327,10 +326,14 @@
         self.p = lax.axis_index("prow")
         self.v = lax.axis_index("pcol")
 
-    def prepare(self, mixed):
+    def prepare(self, mixed, perm):
+        spread = lax.broadcasted_iota(jnp.int32, (256, 256), 0)
         for k in range(2):
-            mixed[k] = dot(self.inverse[k], pick(self.order[k], 256)).astype(jnp.bfloat16)
+            turned = jnp.where(self.order[pl.ds(k, 1), :] == spread, 1.0, 0.0)
+            perm[k] = turned.T.astype(jnp.bfloat16)
+            mixed[k] = dot(self.inverse[k], perm[k]).astype(jnp.bfloat16)
         self.mixed = mixed
+        self.perm = perm
 
     def side_step(self, i, step):
         bf = jnp.bfloat16
@@ -394,7 +397,7 @@
 
         @pl.when(p < 2)
         def _():
-            part = pick(self.order[0, pl.ds(p * 128, 128)], 128)
+            part = self.perm[0, pl.ds(p * 128, 128)]
 
             @pl.loop(0, cols, step=step)
             def _(c):
@@ -404,7 +407,7 @@
 
         @pl.when(jnp.logical_and(p >= 2, p < 4))
         def _():
-            part = pick(self.order[1, pl.ds((p - 2) * 128, 128)], 128)
+            part = self.perm[1, pl.ds((p - 2) * 128, 128)]
 
             @pl.loop(0, cols, step=step)
             def _(c):
@@ -441,8 +444,11 @@
     is_upper = listed & (tile_row < 4)
     is_side = listed & (tile_col < 4)
     side_key = local_row * 2 + tile_col % 2
-    slot_r = slot_lookup(jnp.where(is_upper, local_col, -1), cols)
-    slot_l = slot_lookup(jnp.where(is_side, side_key, -1), 2 * ROW_TILES)
+    targets = jnp.arange(cols + 2 * ROW_TILES, dtype=jnp.int32)[:, None]
+    upper_key = jnp.where(is_upper, local_col, -1)[None, :]
+    lower_key = jnp.where(is_side, cols + side_key, -1)[None, :]
+    match = jnp.where(targets < cols, upper_key, lower_key) == targets
+    found = jnp.sum(jnp.where(match, jnp.arange(slots, dtype=jnp.int32)[None, :], 0), axis=1)
     done = jnp.where(is_upper, local_col, cols + side_key)
     kind = jnp.where(listed, jnp.where(is_upper | is_side, 1, 0), 2)
     done = jnp.where(kind == 1, done, 0)
@@ -452,14 +458,17 @@
     smem = pl.BlockSpec(memory_space=pltpu.SMEM)
     vmem = pl.BlockSpec(memory_space=pltpu.VMEM)
     dma = pltpu.SemaphoreType.DMA
-    n = CHUNKS
+    n = cols
     panel = 2 * edge
     return pl.pallas_call(
         functools.partial(exchange, nz, nbits, cols),
         out_shape=jax.ShapeDtypeStruct(tiles.shape, bf),
-        in_specs=[smem, smem, smem, vmem, vmem, vmem],
+        in_specs=[smem, smem, vmem, pl.BlockSpec(memory_space=pl.ANY), pl.BlockSpec(memory_space=pl.ANY)],
         out_specs=vmem,
         scratch_shapes=[
+            pltpu.VMEM(tiles.shape, bf),
+            pltpu.VMEM((2, panel, panel), bf),
+            pltpu.VMEM((2, panel, panel), bf),
             pltpu.VMEM((cols, 4, edge, edge), bf),
             pltpu.VMEM((2, ROW_TILES, 2, edge, edge), bf),
             pltpu.VMEM((2, 2, edge, edge), bf),
@@ -470,12 +479,12 @@
             pltpu.VMEM((2, panel, panel), bf),
             pltpu.VMEM((panel, panel), bf),
             dma((2, n)), dma((2, n)), dma((2, n)), dma((2, n)), dma((2, n)),
-            dma((2, nbits, SIDE_CHUNKS)), dma((2, SIDE_CHUNKS)), dma((5,)), dma((nbits,)), dma((1,)),
+            dma((2, nbits, SIDE_CHUNKS)), dma((2, SIDE_CHUNKS)), dma((5,)), dma((nbits,)), dma((1,)), dma((2,)),
         ],
         compiler_params=pltpu.CompilerParams(
             collective_id=0, has_side_effects=True, vmem_limit_bytes=48 * 1024 * 1024),
         name="exchange",
-    )(slot_r, slot_l, place, pivots.reshape(2, panel, 1), inverses, tiles)
+    )(found, place, pivots, inverses, tiles)
 
 
 def solution(mesh):

time: 124 us -> 128 us (1.032)
  the two profiles are of different devices: /device:TPU:28 before, /device:TPU:25 now
where the time goes in v5:
time: 128 us
  Pallas kernels  122 us (95%)
  local copies, waits for them, and re-layouts  3.64 us (3%)
  other arithmetic  1.75 us (1%)
    pallas_call x1, Pallas kernels, local(): pl.pallas_call(functools.partial(exchange, nz, nbits, cols), out_shape=ja...  122 us
    unnamed x5, local copies, waits for them, and re-layouts  3.64 us

profile of v5, /device:TPU:25, one launch (start us, length us, event | category | flops | bytes accessed | tf_op | source)
XLA Modules:
  0.0 127.7 jit_solution(5068820102352124985)
XLA Ops:
  0.0 0.8 and_select_fusion.9
  0.8 0.2 select_reduce_fusion.slots
  1.0 0.8 compare_select_fusion
  1.8 0.0 copy-start
  1.8 0.9 copy-done
  2.7 0.0 copy-start.1
  2.7 0.7 copy-done.1
  3.4 122.3 %exchange.1 = bf16[128,128,128]{2,1,0:T(8,128)(2,1)S(1)} custom-call(s32[128]{0:T(128)S(1)} %select_reduce_fusion.slots, s32[4,128]{1,0:T(4,128)S(1)} %pad_add_fusion.place, s32[2,256]{1,0:T(2,128)S(1)} %copy-done.1, bf16[2,256,256]{2,1,0:T(8,128)(2,1)S(1)} %copy-done, bf16[128,128,128]{2,1,0:T(8,128)(2,1)} %tiles_in.1), custom_call_target="tpu_custom_call" | custom-call | tf_op jit(solution)/shard_map/exchange/pallas_call | solution.py:463
  125.7 2.0 %copy.6 = bf16[128,128,128]{2,1,0:T(8,128)(2,1)} copy(bf16[128,128,128]{2,1,0:T(8,128)(2,1)S(1)} %exchange.1) | data formatting | bytes 8388608
  (2 shorter events, 0.0 us)
Async XLA Ops:
  1.8 1.0 copy-start
  2.7 0.7 copy-start.1

commit v6 on v5

--- a/solution.py
+++ b/solution.py
@@ -7,7 +7,10 @@
 from jax.sharding import PartitionSpec as P
 
 ROW_TILES = 32
-AHEAD = 3
+CHUNKS = 32
+AHEAD = (8, 5)
+SKEW = 3
+WINDOW = 3
 GROUP = 16
 SIDE_CHUNKS = 16
 MESH = pl.DeviceIdType.MESH
@@ -26,9 +29,9 @@
     z = p // 2
     core = p % 2
     other = p + 1 - 2 * core
-    n = cols
-    cw = 1
-    stretch = max(n // 32, 1)
+    n = CHUNKS
+    cw = cols // n
+    stretch = 1
     ns = SIDE_CHUNKS
     rw = ROW_TILES // ns
     step = 4
@@ -215,7 +218,7 @@
             side_forward(s, at)
 
     for k in range(2):
-        for j in range(AHEAD):
+        for j in range(AHEAD[k]):
             own(k, j)
 
     @pl.when(v < 2)
@@ -228,18 +231,31 @@
     load_inverse.wait()
     panels.prepare(mixed, perm)
 
+    def turn(k, j):
+        @pl.when(z != k)
+        def _():
+            up(k, j).wait_recv()
+            forward(k, j)
+
+    for j in range(SKEW):
+        turn(1, j)
+
     @pl.loop(0, n)
     def _(j):
-        @pl.when(j + AHEAD < n)
-        def _():
-            own(0, j + AHEAD)
-            own(1, j + AHEAD)
-
-        for k in (1, 0):
-            @pl.when(z != k)
-            def _():
-                up(k, j).wait_recv()
-                forward(k, j)
+        for k in range(2):
+            @pl.when(j + AHEAD[k] < n)
+            def _():
+                own(k, j + AHEAD[k])
+
+        @pl.when(j + SKEW < n)
+        def _():
+            turn(1, j + SKEW)
+
+        turn(0, j)
+
+        @pl.when(jnp.logical_and(z == 1, jnp.logical_and(goes_up(0), j >= WINDOW)))
+        def _():
+            up(0, j - WINDOW).wait_send()
 
         side_turns(j)
 
@@ -280,7 +296,11 @@
     @pl.loop(0, n)
     def _(j):
         for k in range(2):
-            @pl.when(goes_up(k))
+            left = goes_up(k)
+            if k == 0:
+                left = jnp.logical_and(left, jnp.logical_or(z != 1, j >= n - WINDOW))
+
+            @pl.when(left)
             def _():
                 up(k, j).wait_send()
 
@@ -458,7 +478,7 @@
     smem = pl.BlockSpec(memory_space=pltpu.SMEM)
     vmem = pl.BlockSpec(memory_space=pltpu.VMEM)
     dma = pltpu.SemaphoreType.DMA
-    n = cols
+    n = CHUNKS
     panel = 2 * edge
     return pl.pallas_call(
         functools.partial(exchange, nz, nbits, cols),

time: 128 us -> 123 us (0.961)
  the two profiles are of different devices: /device:TPU:25 before, /device:TPU:28 now
where the time goes in v6:
time: 123 us; the launch traced here: 121 us
  Pallas kernels  116 us (94%)
  local copies, waits for them, and re-layouts  3.64 us (3%)
  other arithmetic  1.75 us (1%)
    pallas_call x1, Pallas kernels, local(): pl.pallas_call(functools.partial(exchange, nz, nbits, cols), out_shape=ja...  116 us
    unnamed x5, local copies, waits for them, and re-layouts  3.64 us

profile of v6, /device:TPU:28, one launch (start us, length us, event | category | flops | bytes accessed | tf_op | source)
XLA Modules:
  0.0 121.0 jit_solution(981128350305004972)
XLA Ops:
  0.0 0.8 and_select_fusion.9
  0.8 0.2 select_reduce_fusion.slots
  1.0 0.8 compare_select_fusion
  1.8 0.0 copy-start
  1.8 0.9 copy-done
  2.7 0.0 copy-start.1
  2.7 0.7 copy-done.1
  3.4 115.6 %exchange.1 = bf16[128,128,128]{2,1,0:T(8,128)(2,1)S(1)} custom-call(s32[128]{0:T(128)S(1)} %select_reduce_fusion.slots, s32[4,128]{1,0:T(4,128)S(1)} %pad_add_fusion.place, s32[2,256]{1,0:T(2,128)S(1)} %copy-done.1, bf16[2,256,256]{2,1,0:T(8,128)(2,1)S(1)} %copy-done, bf16[128,128,128]{2,1,0:T(8,128)(2,1)} %tiles_in.1), custom_call_target="tpu_custom_call" | custom-call | tf_op jit(solution)/shard_map/exchange/pallas_call | solution.py:483
  119.0 2.0 %copy.6 = bf16[128,128,128]{2,1,0:T(8,128)(2,1)} copy(bf16[128,128,128]{2,1,0:T(8,128)(2,1)S(1)} %exchange.1) | data formatting | bytes 8388608
  (2 shorter events, 0.0 us)
Async XLA Ops:
  1.8 1.0 copy-start
  2.7 0.7 copy-start.1

commit v7 on v6

--- a/solution.py
+++ b/solution.py
@@ -37,7 +37,7 @@
     step = 4
     per = step // cw
     row_lag = 4 * stretch * ((3 * nbits + 2 * nz + 1) // 4)
-    catch_up = per * (row_lag - 1) // (per - 1)
+    catch_up = per * (row_lag - 2) // (per - 1)
     panels = Panels(cols, order, inverse, rows, side, ext_r, ext_c, tiles, out, mix, both, final, place)
     panels.lead = lead
 
@@ -179,9 +179,7 @@
 
         @pl.when(jnp.logical_and(live, jnp.logical_and(at >= 0, at < ns)))
         def _():
-            @pl.when(at % (step // rw) == 0)
-            def _():
-                panels.side_step(at * rw, step)
+            panels.side_step(at * rw, rw)
 
         @pl.when(j == row_lag)
         def _():
@@ -192,7 +190,7 @@
 
         early = jnp.logical_and(j >= row_lag, j <= catch_up)
         late = jnp.logical_and(j > catch_up, j % per == 0)
-        first = per * jnp.where(j <= catch_up, j - row_lag, j // per - 1)
+        first = per * jnp.where(j <= catch_up, j - row_lag, j // per - 2)
 
         @pl.when(jnp.logical_and(jnp.logical_or(early, late), first < n))
         def _():

time: 123 us -> 122 us (level)
  no operation moved by 1% of the time
where the time goes in v7:
time: 122 us; the launch traced here: 120 us
  Pallas kernels  115 us (94%)
  local copies, waits for them, and re-layouts  3.64 us (3%)
  other arithmetic  1.75 us (1%)
    pallas_call x1, Pallas kernels, local(): pl.pallas_call(functools.partial(exchange, nz, nbits, cols), out_shape=ja...  115 us
    unnamed x5, local copies, waits for them, and re-layouts  3.64 us

profile of v7, /device:TPU:28, one launch (start us, length us, event | category | flops | bytes accessed | tf_op | source)
XLA Modules:
  0.0 120.3 jit_solution(13809180030039800576)
XLA Ops:
  0.0 0.8 and_select_fusion.9
  0.8 0.2 select_reduce_fusion.slots
  1.0 0.8 compare_select_fusion
  1.8 0.0 copy-start
  1.8 0.9 copy-done
  2.7 0.0 copy-start.1
  2.7 0.7 copy-done.1
  3.4 114.8 %exchange.1 = bf16[128,128,128]{2,1,0:T(8,128)(2,1)S(1)} custom-call(s32[128]{0:T(128)S(1)} %select_reduce_fusion.slots, s32[4,128]{1,0:T(4,128)S(1)} %pad_add_fusion.place, s32[2,256]{1,0:T(2,128)S(1)} %copy-done.1, bf16[2,256,256]{2,1,0:T(8,128)(2,1)S(1)} %copy-done, bf16[128,128,128]{2,1,0:T(8,128)(2,1)} %tiles_in.1), custom_call_target="tpu_custom_call" | custom-call | tf_op jit(solution)/shard_map/exchange/pallas_call | solution.py:481
  118.2 2.0 %copy.6 = bf16[128,128,128]{2,1,0:T(8,128)(2,1)} copy(bf16[128,128,128]{2,1,0:T(8,128)(2,1)S(1)} %exchange.1) | data formatting | bytes 8388608
  (2 shorter events, 0.0 us)
Async XLA Ops:
  1.8 1.0 copy-start
  2.7 0.7 copy-start.1

commit v8 on v7

--- a/solution.py
+++ b/solution.py
@@ -11,7 +11,7 @@
 AHEAD = (8, 5)
 SKEW = 3
 WINDOW = 3
-GROUP = 16
+GROUP = 32
 SIDE_CHUNKS = 16
 MESH = pl.DeviceIdType.MESH
 

time: 122 us -> 122 us (level)
  no operation moved by 1% of the time
where the time goes in v8:
time: 122 us; the launch traced here: 120 us
  Pallas kernels  114 us (93%)
  local copies, waits for them, and re-layouts  3.64 us (3%)
  other arithmetic  1.75 us (1%)
    pallas_call x1, Pallas kernels, local(): pl.pallas_call(functools.partial(exchange, nz, nbits, cols), out_shape=ja...  114 us
    unnamed x5, local copies, waits for them, and re-layouts  3.64 us

profile of v8, /device:TPU:28, one launch (start us, length us, event | category | flops | bytes accessed | tf_op | source)
XLA Modules:
  0.0 119.6 jit_solution(10640772383685274043)
XLA Ops:
  0.0 0.8 and_select_fusion.9
  0.8 0.2 select_reduce_fusion.slots
  1.0 0.8 compare_select_fusion
  1.8 0.0 copy-start
  1.8 0.9 copy-done
  2.7 0.0 copy-start.1
  2.7 0.7 copy-done.1
  3.4 114.2 %exchange.1 = bf16[128,128,128]{2,1,0:T(8,128)(2,1)S(1)} custom-call(s32[128]{0:T(128)S(1)} %select_reduce_fusion.slots, s32[4,128]{1,0:T(4,128)S(1)} %pad_add_fusion.place, s32[2,256]{1,0:T(2,128)S(1)} %copy-done.1, bf16[2,256,256]{2,1,0:T(8,128)(2,1)S(1)} %copy-done, bf16[128,128,128]{2,1,0:T(8,128)(2,1)} %tiles_in.1), custom_call_target="tpu_custom_call" | custom-call | tf_op jit(solution)/shard_map/exchange/pallas_call | solution.py:481
  117.6 2.0 %copy.6 = bf16[128,128,128]{2,1,0:T(8,128)(2,1)} copy(bf16[128,128,128]{2,1,0:T(8,128)(2,1)S(1)} %exchange.1) | data formatting | bytes 8388608
  (2 shorter events, 0.0 us)
Async XLA Ops:
  1.8 1.0 copy-start
  2.7 0.7 copy-start.1
